TPU v7x, 32 devices: a whole 2x2x4 slice. The times are simulated.
32 devices in a mesh: groups: 2 (over y), layer: 4 (over z), ex: 4 (over x, core).
Axes of the slice: x: 2, y: 2, z: 4, core: 2. Of those that a mesh axis runs over, the one named last changes fastest.
Arguments:
- acts: bfloat16 [4, 8, 256, 4096], P('layer', ('groups', 'ex')), parts along dimension 1, may hold values from -6 to 6
- grads: bfloat16 [4, 8, 256, 1024], P('layer', ('groups', 'ex')), parts along dimension 1, may hold values from -6 to 6
- proj_in: bfloat16 [4, 128, 4096], P('layer'), may hold values from -0.09375 to 0.09375
- proj_out: bfloat16 [4, 128, 1024], P('layer'), may hold values from -0.1875 to 0.1875
- queries: bfloat16 [512, 16384], P('layer', 'ex'), may hold values from -0.046875 to 0.046875
Outputs:
- scores: float32 [8, 512], P(('groups', 'ex'), 'layer'), parts along dimension 0
There are 2 independent parts, one for each index of `groups`. A program takes and returns all parts, laid end to end along the dimension named above; an argument that names none is the same for every part. Nothing has to cross between parts.
All inputs are finite; a program needn't handle non-finite values.
Results may differ from a plain program's by a relative error of at most 0.005.
Values may be sent and summed in bfloat16 or wider, within the bound.
No kernel may reach another device: no remote copies, remote signals or barrier semaphores. Data moves between devices by JAX's collectives and lax.ppermute only.
A program may use at most 64 MiB of HBM per device.

v0:
```python
import math

import jax
import jax.numpy as jnp
from jax import lax
from jax.sharding import PartitionSpec as P


def project_rows(rows, weight):
    return lax.dot_general(
        rows, weight, (((1,), (1,)), ((), ())), preferred_element_type=jnp.float32
    )


def on_device(acts, grads, proj_in, proj_out, queries):
    layers = lax.axis_size("layer")
    inputs = acts[0]
    outputs = grads[0]
    count, tokens, width_in = inputs.shape
    width_out = outputs.shape[2]
    x_low = project_rows(inputs.reshape(count * tokens, width_in), proj_in[0]).astype(jnp.bfloat16)
    g_low = project_rows(outputs.reshape(count * tokens, width_out), proj_out[0]).astype(
        jnp.bfloat16
    )
    k_in = x_low.shape[1]
    k_out = g_low.shape[1]
    outer = jnp.einsum(
        "esa,esb->eab",
        g_low.reshape(count, tokens, k_out),
        x_low.reshape(count, tokens, k_in),
        preferred_element_type=jnp.float32,
    )
    partial_value = outer.reshape(count, k_out * k_in)
    scale = 1.0 / math.sqrt(tokens * layers)
    shares = lax.psum_scatter(partial_value, "layer", scatter_dimension=1, tiled=True)
    feat_low = lax.all_gather(shares.astype(jnp.bfloat16), "layer", axis=1, tiled=True)
    raw = project_rows(feat_low, lax.all_gather(queries, "ex", axis=1, tiled=True))
    return raw * scale


def solution(mesh):
    placed = (
        P("layer", ("groups", "ex"), None, None),
        P("layer", ("groups", "ex"), None, None),
        P("layer", None, None),
        P("layer", None, None),
        P("layer", "ex"),
    )
    return jax.shard_map(
        on_device,
        mesh=mesh,
        in_specs=placed,
        out_specs=P(("groups", "ex"), "layer"),
        check_vma=False,
    )
```

profile of v0, /device:TPU:0, one launch (start us, length us, event | category | flops | bytes accessed | tf_op | source)
XLA Modules:
  0.0 192.2 jit_solution(18384919878159665780)
XLA Ops:
  7.4 0.0 copy-start
  7.4 0.0 reduce-scatter.4.cloned.1.call-start
  7.4 1.6 copy-done
  9.0 1.9 %fusion.2 = bf16[256,128]{1,0:T(8,128)(2,1)S(1)} fusion(bf16[1,1,256,4096]{3,2,1,0:T(8,128)(2,1)S(1)} %copy-done, bf16[1,128,4096]{2,1,0:T(8,128)(2,1)} %param.7), kind=kOutput, calls=%fused_computation.2 | convolution fusion | flops 268468224 | bytes 3211264 | tf_op jit(solution)/shard_map/dot_general | solution.py:10
  10.9 1.6 fusion.5
  12.5 4.9 %copy.6 = f32[1,16384]{0,1:T(8,128)} copy(f32[1,16384]{1,0:T(1,128)S(1)} %bitcast.34) | data formatting | bytes 131072
  17.4 0.0 reduce-scatter.4.cloned.1.call-update
  17.4 0.0 all-gather.2.cloned.1.call-start
  17.5 0.5 all-gather.2.cloned.1.call-update
  18.0 146.7 %reduce-scatter.4.cloned.1.call-done = f32[4096,1]{1,0:T(8,128)} async-done(((f32[16384,1]{1,0:T(8,128)}), f32[4096,1]{1,0:T(8,128)}) %reduce-scatter.4.cloned.1.call-update) | async-done | bytes 16400
  164.7 2.2 %copy.7 = bf16[1,4096]{1,0:T(2,128)(2,1)S(1)} copy(f32[1,4096]{0,1:T(8,128)} %bitcast.33) | data formatting | bytes 24576
  166.9 13.9 %all_gather.6 = bf16[1,16384]{1,0:T(2,128)(2,1)S(1)} all-gather(bf16[1,4096]{1,0:T(2,128)(2,1)S(1)} %copy.7), channel_id=1, replica_groups=mesh['groups'=2,'layer'=4,'ex'=4] {'layer'}, dimensions={1}, use_global_device_ids=true | all-gather | bytes 40960 | tf_op jit(solution)/shard_map/all_gather | solution.py:36
  180.9 0.0 all-gather.2.cloned.1.call-done
  180.9 3.9 %fusion.7 = f32[1,128]{1,0:T(1,128)} fusion(bf16[128,16384]{1,0:T(8,128)(2,1)} %all-gather.2.cloned.1.call-done, bf16[1,16384]{1,0:T(2,128)(2,1)S(1)} %all_gather.6), kind=kOutput, calls=%fused_computation.7 | convolution fusion | flops 4194432 | bytes 4227584 | tf_op jit(solution)/shard_map/dot_general | solution.py:10
Async XLA Ops:
  7.4 1.6 copy-start
  7.4 157.4 %reduce-scatter.4.cloned.1.call-start = ((), (), s32[]{:S(2)}) async-start(), calls=%async_computation.2 | async-start | bytes 10485760
  17.4 163.5 %all-gather.2.cloned.1.call-start = ((), (), s32[]{:S(2)}) async-start(), calls=%async_computation.1 | async-start | bytes 5242880 | tf_op jit(solution)/shard_map/all_gather | solution.py:37
Sparse Core Ops, SparseCore 0:
  17.5 147.1 reduce-scatter.3
Sparse Core Ops, SparseCore 1:
  19.5 37.0 all-gather.1
where the time goes:
time: 192 us
  waiting for transfers between devices  147 us (77%)
  between operations  14.9 us (8%)
  blocking collectives  13.9 us (7%)
  local copies, waits for them, and re-layouts  8.68 us (5%)
  matrix products  7.43 us (4%)
    unnamed x3, waiting for transfers between devices  147 us
    all_gather x1, blocking collectives, on_device(): lax.all_gather(shares.astype(jnp.bfloat16), 'layer', axis=1, tiled=True)  13.9 us
    unnamed x4, local copies, waits for them, and re-layouts  8.68 us
    dot_general x2, matrix products, project_rows(): lax.dot_general(rows, weight, (((1,), (1,)), ((), ())), preferred_element...  5.82 us
  transfers between devices with their start and end apart: 2, of which 1 were waited for; matrix products, arithmetic and copies ran while one was open for 1% of the time, Pallas kernels for 0%

commit v1 on v0

v1 whole, which is shorter than its diff:
```python
import math

import jax
import jax.numpy as jnp
from jax import lax
from jax.experimental import pallas as pl
from jax.experimental.pallas import tpu as pltpu
from jax.sharding import PartitionSpec as P

LANES = 128
PIECES = 4
VMEM_SPEC = pl.BlockSpec(memory_space=pltpu.VMEM)
ANY_SPEC = pl.BlockSpec(memory_space=pl.ANY)


def dot_nt(rows, weight):
    return lax.dot_general(
        rows, weight, (((1,), (1,)), ((), ())), preferred_element_type=jnp.float32
    )


def outer_kernel(acts, grads, proj_in, proj_out, low_ref, full_ref, a_buf, g_buf, pi_buf, po_buf, sems):
    width = acts.shape[1] // PIECES
    grad_copies = [
        pltpu.make_async_copy(proj_out, po_buf, sems.at[0]),
        pltpu.make_async_copy(grads, g_buf, sems.at[1]),
    ]
    act_copies = []
    for k in range(PIECES):
        cols = pl.ds(k * width, width)
        act_copies.append((
            pltpu.make_async_copy(proj_in.at[:, cols], pi_buf.at[:, cols], sems.at[2 + 2 * k]),
            pltpu.make_async_copy(acts.at[:, cols], a_buf.at[:, cols], sems.at[3 + 2 * k]),
        ))
    for copy in grad_copies:
        copy.start()
    for pair in act_copies:
        for copy in pair:
            copy.start()
    for copy in grad_copies:
        copy.wait()
    g_low = dot_nt(po_buf[...], g_buf[...]).astype(jnp.bfloat16)
    x_low = None
    for k, pair in enumerate(act_copies):
        for copy in pair:
            copy.wait()
        cols = slice(k * width, (k + 1) * width)
        part = dot_nt(a_buf[:, cols], pi_buf[:, cols])
        x_low = part if x_low is None else x_low + part
    outer = jnp.dot(g_low, x_low.astype(jnp.bfloat16), preferred_element_type=jnp.float32)
    full_ref[...] = outer
    low_ref[...] = outer.astype(jnp.bfloat16)


def outer_product(acts, grads, proj_in, proj_out):
    k_in, k_out = proj_in.shape[0], proj_out.shape[0]
    return pl.pallas_call(
        outer_kernel,
        out_shape=(
            jax.ShapeDtypeStruct((k_out, k_in), jnp.bfloat16),
            jax.ShapeDtypeStruct((k_out, k_in), jnp.float32),
        ),
        in_specs=[ANY_SPEC] * 4,
        out_specs=(VMEM_SPEC, VMEM_SPEC),
        scratch_shapes=[
            pltpu.VMEM(acts.shape, jnp.bfloat16),
            pltpu.VMEM(grads.shape, jnp.bfloat16),
            pltpu.VMEM(proj_in.shape, jnp.bfloat16),
            pltpu.VMEM(proj_out.shape, jnp.bfloat16),
            pltpu.SemaphoreType.DMA((2 + 2 * PIECES,)),
        ],
        compiler_params=pltpu.CompilerParams(vmem_limit_bytes=16 * 2**20),
    )(acts, grads, proj_in, proj_out)


def spread_kernel(count, own, got, *outs):
    me = lax.axis_index("ex")
    rows = own.shape[0] // count
    for m in range(count):
        block = pl.ds(pl.multiple_of((me ^ m) * rows, rows), rows)
        outs[m][...] = (own[block, :] + got[block, :].astype(jnp.float32)).astype(jnp.bfloat16)


def spread(own, got, count):
    rows = own.shape[0] // count
    return pl.pallas_call(
        lambda *refs: spread_kernel(count, *refs),
        out_shape=[jax.ShapeDtypeStruct((rows, own.shape[1]), jnp.bfloat16)] * count,
        in_specs=[VMEM_SPEC] * 2,
        out_specs=[VMEM_SPEC] * count,
    )(own, got)


def score_kernel(count, queries, *refs):
    feats, outs = refs[:count], refs[count:]
    table = jnp.stack([f[...].astype(jnp.float32) for f in feats], axis=0)
    table = jnp.swapaxes(table, 0, 1)
    table = jnp.concatenate([table[a] for a in range(table.shape[0])], axis=1)
    raw = dot_nt(table.astype(jnp.bfloat16), queries[...])
    for m in range(count):
        outs[m][...] = raw[m:m + 1]


def score(queries, feats):
    count = len(feats)
    return pl.pallas_call(
        lambda *refs: score_kernel(count, *refs),
        out_shape=[jax.ShapeDtypeStruct((1, queries.shape[0]), jnp.float32)] * count,
        in_specs=[VMEM_SPEC] * (count + 1),
        out_specs=[VMEM_SPEC] * count,
        compiler_params=pltpu.CompilerParams(vmem_limit_bytes=16 * 2**20),
    )(queries, *feats)


def swap(value, axis, bit):
    size = lax.axis_size(axis)
    return lax.ppermute(value, axis, [(s, s ^ bit) for s in range(size)])


def on_device(acts, grads, proj_in, proj_out, queries):
    layers, count = lax.axis_size("layer"), lax.axis_size("ex")
    tokens = acts.shape[2]
    low, full = outer_product(acts[0, 0], grads[0, 0], proj_in[0], proj_out[0])
    bit = 1
    while bit * 2 < layers:
        full = full + swap(low, "layer", bit).astype(jnp.float32)
        low = full.astype(jnp.bfloat16)
        bit *= 2
    blocks = spread(full, swap(low, "layer", bit), count)
    order = sorted(range(1, count), reverse=True)
    got = {m: swap(blocks[m], "ex", m) for m in order}
    parts = score(queries, [blocks[0]] + [got[m] for m in range(1, count)])
    back = {m: swap(parts[m], "ex", m) for m in order}
    raw = parts[0]
    for m in range(1, count):
        raw = raw + back[m]
    return raw * (1.0 / math.sqrt(tokens * layers))


def solution(mesh):
    placed = (
        P("layer", ("groups", "ex"), None, None),
        P("layer", ("groups", "ex"), None, None),
        P("layer", None, None),
        P("layer", None, None),
        P("layer", "ex"),
    )
    return jax.shard_map(
        on_device,
        mesh=mesh,
        in_specs=placed,
        out_specs=P(("groups", "ex"), "layer"),
        check_vma=False,
    )
```

time: 192 us -> 30.5 us (0.16)
  waiting for transfers between devices: 147 us -> 8.83 us
  between operations: 14.9 us -> 0.03 us
  blocking collectives: 13.9 us -> 0 us
  starting transfers between devices: 0.05 us -> 9.97 us
  matrix products: 7.43 us -> 0 us
  Pallas kernels: 0 us -> 4.08 us
  local copies, waits for them, and re-layouts: 8.68 us -> 6.11 us
    unnamed x3 -> x0, waiting for transfers between devices: 147 us -> none
    all_gather x1 -> x0, blocking collectives: 13.9 us -> none  [on_device(): lax.all_gather(shares.astype(jnp.bfloat16), 'layer', axis=1, tiled=True)]
    ppermute x0 -> x8, starting transfers between devices: none -> 9.97 us  [swap(): return lax.ppermute(value, axis, [(s, s ^ bit) for s in range(size)])]
    ppermute x0 -> x8, waiting for transfers between devices: none -> 8.83 us  [swap(): return lax.ppermute(value, axis, [(s, s ^ bit) for s in range(size)])]
    dot_general x3 -> x0, matrix products: 7.43 us -> none  [the longest x2 5.82 us: project_rows(): lax.dot_general(rows, weight, (((1,), (1,)), ((), ())), preferred_element...]
    pallas_call x0 -> x3, Pallas kernels: none -> 4.08 us  [the longest x1 2.25 us: outer_product(): pl.pallas_call(outer_kernel, out_shape=(jax.ShapeDtypeStruct((k_out, k_in...]
    unnamed x4 -> x14, local copies, waits for them, and re-layouts: 8.68 us -> 6.11 us
  transfers between devices with their start and end apart: 2 -> 8, of which waited for: 1 -> 5; matrix products, arithmetic and copies ran while one was open for 1% -> 0% of each run, Pallas kernels for 0% -> 0%
where the time goes in v1:
time: 30.5 us; the launch traced here: 30.2 us
  starting transfers between devices  9.97 us (33%)
  waiting for transfers between devices  8.83 us (29%)
  local copies, waits for them, and re-layouts  6.11 us (20%)
  Pallas kernels  4.08 us (13%)
  other arithmetic  1.16 us (4%)
    ppermute x8, starting transfers between devices, swap(): return lax.ppermute(value, axis, [(s, s ^ bit) for s in range(size)])  9.97 us
    ppermute x8, waiting for transfers between devices, swap(): return lax.ppermute(value, axis, [(s, s ^ bit) for s in range(size)])  8.83 us
    unnamed x14, local copies, waits for them, and re-layouts  6.11 us
    pallas_call x1, Pallas kernels, outer_product(): pl.pallas_call(outer_kernel, out_shape=(jax.ShapeDtypeStruct((k_out, k_in...  2.25 us
    pallas_call x1, Pallas kernels, spread(): pl.pallas_call(lambda *refs: spread_kernel(count, *refs), out_shape=[jax....  1.45 us
    convert_element_type x1, other arithmetic, on_device(): low = full.astype(jnp.bfloat16)  0.65 us
  transfers between devices with their start and end apart: 8, of which 5 were waited for; matrix products, arithmetic and copies ran while one was open for 0% of the time, Pallas kernels for 0%

profile of v1, /device:TPU:0, one launch (start us, length us, event | category | flops | bytes accessed | tf_op | source)
XLA Modules:
  0.0 30.2 jit_solution(12531358829218559081)
XLA Ops:
  0.0 0.0 copy-start
  0.0 1.6 %copy-done = bf16[1,1,256,4096]{3,2,1,0:T(8,128)(2,1)S(1)} copy-done((bf16[1,1,256,4096]{3,2,1,0:T(8,128)(2,1)S(1)}, bf16[1,1,256,4096]{3,2,1,0:T(8,128)(2,1)}, u32[]{:S(2)}) %copy-start) | copy-done | bytes 2097176
  1.6 1.2 %copy-done.2 = bf16[1,128,4096]{2,1,0:T(8,128)(2,1)S(1)} copy-done((bf16[1,128,4096]{2,1,0:T(8,128)(2,1)S(1)}, bf16[1,128,4096]{2,1,0:T(8,128)(2,1)}, u32[]{:S(2)}) %copy-start.2) | copy-done | bytes 1048600
  2.8 0.0 copy-start.3
  2.8 1.0 %copy-done.3 = bf16[1,1,256,1024]{3,2,1,0:T(8,128)(2,1)S(1)} copy-done((bf16[1,1,256,1024]{3,2,1,0:T(8,128)(2,1)S(1)}, bf16[1,1,256,1024]{3,2,1,0:T(8,128)(2,1)}, u32[]{:S(2)}) %copy-start.3) | copy-done | bytes 524312
  3.9 0.0 copy-start.4
  3.9 0.9 %copy-done.4 = bf16[1,128,1024]{2,1,0:T(8,128)(2,1)S(1)} copy-done((bf16[1,128,1024]{2,1,0:T(8,128)(2,1)S(1)}, bf16[1,128,1024]{2,1,0:T(8,128)(2,1)}, u32[]{:S(2)}) %copy-start.4) | copy-done | bytes 262168
  4.8 0.0 copy-start.1
  4.8 2.3 %shard_map.55 = (bf16[128,128]{1,0:T(8,128)(2,1)S(1)}, f32[128,128]{1,0:T(8,128)S(1)}) custom-call(bf16[256,4096]{1,0:T(8,128)(2,1)S(1)} %bitcast.4, bf16[256,1024]{1,0:T(8,128)(2,1)S(1)} %bitcast.6, bf16[128,4096]{1,0:T(8,128)(2,1)S(1)} %bitcast.5, bf16[128,1024]{1,0:T(8,128)(2,1)S(1)} %bitcast.7), custom_call_target="tpu_custom_call" | custom-call | tf_op jit(solution)/shard_map/pallas_call | solution.py:57
  7.1 3.1 %collective-permute-start = (bf16[128,128]{1,0:T(8,128)(2,1)S(1)}, bf16[128,128]{1,0:T(8,128)(2,1)S(1)}, u32[]{:S(2)}, u32[]{:S(2)}) collective-permute-start(bf16[128,128]{1,0:T(8,128)(2,1)S(1)} %get-tuple-element.16), channel_id=1, source_target_pairs={{0,4},{4,0},{8,12},{12,8},{1,5},{5,1},{9,13},{13,9},{2,6},{6,2},{1... | collective-permute-start | bytes 98312 | tf_op jit(solution)/shard_map/ppermute | solution.py:117
  10.2 1.9 %collective-permute-done = bf16[128,128]{1,0:T(8,128)(2,1)S(1)} collective-permute-done((bf16[128,128]{1,0:T(8,128)(2,1)S(1)}, bf16[128,128]{1,0:T(8,128)(2,1)S(1)}, u32[]{:S(2)}, u32[]{:S(2)}) %collective-permute-start) | collective-permute-done | bytes 32800 | tf_op jit(solution)/shard_map/ppermute | solution.py:117
  12.1 0.6 %fusion = (bf16[128,128]{1,0:T(8,128)(2,1)S(1)}, f32[128,128]{1,0:T(8,128)}) fusion(f32[128,128]{1,0:T(8,128)S(1)} %get-tuple-element.15, bf16[128,128]{1,0:T(8,128)(2,1)S(1)} %collective-permute-done), kind=kLoop, calls=%fused_computation.2 | loop fusion | flops 49152 | bytes 196608 | tf_op jit(solution)/shard_map/convert_element_type | solution.py:127
  12.7 3.0 %collective-permute-start.1 = (bf16[128,128]{1,0:T(8,128)(2,1)S(1)}, bf16[128,128]{1,0:T(8,128)(2,1)S(1)}, u32[]{:S(2)}, u32[]{:S(2)}) collective-permute-start(bf16[128,128]{1,0:T(8,128)(2,1)S(1)} %get-tuple-element.25), channel_id=1, source_target_pairs={{0,8},{4,12},{8,0},{12,4},{1,9},{5,13},{9,1},{13,5},{2,10},{6,14},... | collective-permute-start | bytes 98312 | tf_op jit(solution)/shard_map/ppermute | solution.py:117
  15.7 1.9 %collective-permute-done.1.refs_1_ = bf16[128,128]{1,0:T(8,128)(2,1)S(1)} collective-permute-done((bf16[128,128]{1,0:T(8,128)(2,1)S(1)}, bf16[128,128]{1,0:T(8,128)(2,1)S(1)}, u32[]{:S(2)}, u32[]{:S(2)}) %collective-permute-start.1) | collective-permute-done | bytes 32800 | tf_op jit(solution)/shard_map/ppermute | solution.py:117
  17.6 0.6 %copy-done.6 = bf16[128,128]{1,0:T(8,128)(2,1)} copy-done((bf16[128,128]{1,0:T(8,128)(2,1)}, bf16[128,128]{1,0:T(8,128)(2,1)S(1)}, u32[]{:S(2)}) %copy-start.6) | copy-done | bytes 32792
  18.2 1.5 %shard_map.56 = (bf16[32,128]{1,0:T(8,128)(2,1)}, bf16[32,128]{1,0:T(8,128)(2,1)}, bf16[32,128]{1,0:T(8,128)(2,1)}, bf16[32,128]{1,0:T(8,128)(2,1)}) custom-call(f32[128,128]{1,0:T(8,128)} %get-tuple-element.26.refs_0_, bf16[128,128]{1,0:T(8,128)(2,1)} %copy-done.6), custom_call_target="tpu_custom_call" | custom-call | tf_op jit(solution)/shard_map/pallas_call | solution.py:86
  19.7 0.0 collective-permute-start.2
  19.7 1.8 %collective-permute-start.3 = (bf16[32,128]{1,0:T(8,128)(2,1)}, bf16[32,128]{1,0:T(8,128)(2,1)S(1)}, u32[]{:S(2)}, u32[]{:S(2)}) collective-permute-start(bf16[32,128]{1,0:T(8,128)(2,1)} %get-tuple-element.19), channel_id=1, source_target_pairs={{0,2},{1,3},{2,0},{3,1},{4,6},{5,7},{6,4},{7,5},{8,10},{9,11},{10,... | collective-permute-start | bytes 24584 | tf_op jit(solution)/shard_map/ppermute | solution.py:117
  21.5 0.1 collective-permute-start.4
  21.7 0.0 collective-permute-done.2.refs_2_
  21.7 1.9 %collective-permute-done.3.refs_3_ = bf16[32,128]{1,0:T(8,128)(2,1)S(1)} collective-permute-done((bf16[32,128]{1,0:T(8,128)(2,1)}, bf16[32,128]{1,0:T(8,128)(2,1)S(1)}, u32[]{:S(2)}, u32[]{:S(2)}) %collective-permute-start.3) | collective-permute-done | bytes 8224 | tf_op jit(solution)/shard_map/ppermute | solution.py:117
  23.6 1.2 %collective-permute-done.4.refs_4_ = bf16[32,128]{1,0:T(8,128)(2,1)S(1)} collective-permute-done((bf16[32,128]{1,0:T(8,128)(2,1)}, bf16[32,128]{1,0:T(8,128)(2,1)S(1)}, u32[]{:S(2)}, u32[]{:S(2)}) %collective-permute-start.4) | collective-permute-done | bytes 8224 | tf_op jit(solution)/shard_map/ppermute | solution.py:117
  24.8 0.0 copy-done.1
  24.8 0.7 %copy-done.5 = bf16[32,128]{1,0:T(8,128)(2,1)S(1)} copy-done((bf16[32,128]{1,0:T(8,128)(2,1)S(1)}, bf16[32,128]{1,0:T(8,128)(2,1)}, u32[]{:S(2)}) %copy-start.5) | copy-done | bytes 8216
  25.5 0.4 %shard_map.57 = (f32[1,128]{1,0:T(1,128)S(1)}, f32[1,128]{1,0:T(1,128)S(1)}, f32[1,128]{1,0:T(1,128)S(1)}, f32[1,128]{1,0:T(1,128)S(1)}) custom-call(bf16[128,4096]{1,0:T(8,128)(2,1)S(1)} %copy-done.1, bf16[32,128]{1,0:T(8,128)(2,1)S(1)} %copy-done.5, bf16[32,128]{1,0:T(8,128)(2,1)S(1)} %collective-permute-done.2.refs_2_, ...), custom_call_target="tpu_custom_call" | custom-call | tf_op jit(solution)/shard_map/pallas_call | solution.py:106
  25.9 0.2 collective-permute-start.5
  26.1 0.5 %collective-permute-start.6 = (f32[1,128]{1,0:T(1,128)S(1)}, f32[1,128]{1,0:T(1,128)S(1)}, u32[]{:S(2)}, u32[]{:S(2)}) collective-permute-start(f32[1,128]{1,0:T(1,128)S(1)} %get-tuple-element.23), channel_id=1, source_target_pairs={{0,2},{1,3},{2,0},{3,1},{4,6},{5,7},{6,4},{7,5},{8,10},{9,11},{10,... | collective-permute-start | bytes 1544 | tf_op jit(solution)/shard_map/ppermute | solution.py:117
  26.6 1.2 %collective-permute-start.7 = (f32[1,128]{1,0:T(1,128)S(1)}, f32[1,128]{1,0:T(1,128)S(1)}, u32[]{:S(2)}, u32[]{:S(2)}) collective-permute-start(f32[1,128]{1,0:T(1,128)S(1)} %get-tuple-element.24), channel_id=1, source_target_pairs={{0,3},{1,2},{2,1},{3,0},{4,7},{5,6},{6,5},{7,4},{8,11},{9,10},{10,... | collective-permute-start | bytes 1544 | tf_op jit(solution)/shard_map/ppermute | solution.py:117
  27.8 0.0 collective-permute-done.5
  27.8 1.9 %collective-permute-done.6 = f32[1,128]{1,0:T(1,128)S(1)} collective-permute-done((f32[1,128]{1,0:T(1,128)S(1)}, f32[1,128]{1,0:T(1,128)S(1)}, u32[]{:S(2)}, u32[]{:S(2)}) %collective-permute-start.6) | collective-permute-done | bytes 544 | tf_op jit(solution)/shard_map/ppermute | solution.py:117
  29.7 0.0 collective-permute-done.7
  29.7 0.5 %add_multiply_fusion = f32[1,128]{1,0:T(1,128)} fusion(f32[1,128]{1,0:T(1,128)S(1)} %collective-permute-done.7, f32[1,128]{1,0:T(1,128)S(1)} %collective-permute-done.6, f32[1,128]{1,0:T(1,128)S(1)} %get-tuple-element.21, f32[1,128]{1,0:T(1,128)S(1)} %collective-permute-done.5), kind=kLoop, calls=%fused_computation.1 | loop fusion | flops 512 | bytes 2560 | tf_op jit(solution)/shard_map/mul | solution.py:137
  (3 shorter events, 0.0 us)
Async XLA Ops:
  0.0 1.6 %copy-start = (bf16[1,1,256,4096]{3,2,1,0:T(8,128)(2,1)S(1)}, bf16[1,1,256,4096]{3,2,1,0:T(8,128)(2,1)}, u32[]{:S(2)}) copy-start(bf16[1,1,256,4096]{3,2,1,0:T(8,128)(2,1)} %param.5) | copy-start | bytes 6291460
  1.6 1.2 %copy-start.2 = (bf16[1,128,4096]{2,1,0:T(8,128)(2,1)S(1)}, bf16[1,128,4096]{2,1,0:T(8,128)(2,1)}, u32[]{:S(2)}) copy-start(bf16[1,128,4096]{2,1,0:T(8,128)(2,1)} %param.7) | copy-start | bytes 3145732
  2.8 1.0 %copy-start.3 = (bf16[1,1,256,1024]{3,2,1,0:T(8,128)(2,1)S(1)}, bf16[1,1,256,1024]{3,2,1,0:T(8,128)(2,1)}, u32[]{:S(2)}) copy-start(bf16[1,1,256,1024]{3,2,1,0:T(8,128)(2,1)} %param.6) | copy-start | bytes 1572868
  3.9 0.9 %copy-start.4 = (bf16[1,128,1024]{2,1,0:T(8,128)(2,1)S(1)}, bf16[1,128,1024]{2,1,0:T(8,128)(2,1)}, u32[]{:S(2)}) copy-start(bf16[1,128,1024]{2,1,0:T(8,128)(2,1)} %param.8) | copy-start | bytes 786436
  4.8 20.0 %copy-start.1 = (bf16[128,4096]{1,0:T(8,128)(2,1)S(1)}, bf16[128,4096]{1,0:T(8,128)(2,1)}, u32[]{:S(2)}) copy-start(bf16[128,4096]{1,0:T(8,128)(2,1)} %refs_0_.1) | copy-start | bytes 3145732
  7.1 5.0 %collective-permute-start = (bf16[128,128]{1,0:T(8,128)(2,1)S(1)}, bf16[128,128]{1,0:T(8,128)(2,1)S(1)}, u32[]{:S(2)}, u32[]{:S(2)}) collective-permute-start(bf16[128,128]{1,0:T(8,128)(2,1)S(1)} %get-tuple-element.16), channel_id=1, source_target_pairs={{0,4},{4,0},{8,12},{12,8},{1,5},{5,1},{9,13},{13,9},{2,6},{6,2},{1... | collective-permute-start | bytes 98312 | tf_op jit(solution)/shard_map/ppermute | solution.py:117
  12.7 4.9 %collective-permute-start.1 = (bf16[128,128]{1,0:T(8,128)(2,1)S(1)}, bf16[128,128]{1,0:T(8,128)(2,1)S(1)}, u32[]{:S(2)}, u32[]{:S(2)}) collective-permute-start(bf16[128,128]{1,0:T(8,128)(2,1)S(1)} %get-tuple-element.25), channel_id=1, source_target_pairs={{0,8},{4,12},{8,0},{12,4},{1,9},{5,13},{9,1},{13,5},{2,10},{6,14},... | collective-permute-start | bytes 98312 | tf_op jit(solution)/shard_map/ppermute | solution.py:117
  17.6 0.6 %copy-start.6 = (bf16[128,128]{1,0:T(8,128)(2,1)}, bf16[128,128]{1,0:T(8,128)(2,1)S(1)}, u32[]{:S(2)}) copy-start(bf16[128,128]{1,0:T(8,128)(2,1)S(1)} %collective-permute-done.1.refs_1_) | copy-start | bytes 98308
  19.7 2.0 %collective-permute-start.2 = (bf16[32,128]{1,0:T(8,128)(2,1)}, bf16[32,128]{1,0:T(8,128)(2,1)S(1)}, u32[]{:S(2)}, u32[]{:S(2)}) collective-permute-start(bf16[32,128]{1,0:T(8,128)(2,1)} %get-tuple-element.18), channel_id=1, source_target_pairs={{0,1},{1,0},{2,3},{3,2},{4,5},{5,4},{6,7},{7,6},{8,9},{9,8},{10,11... | collective-permute-start | bytes 24584 | tf_op jit(solution)/shard_map/ppermute | solution.py:117
  19.7 3.9 %collective-permute-start.3 = (bf16[32,128]{1,0:T(8,128)(2,1)}, bf16[32,128]{1,0:T(8,128)(2,1)S(1)}, u32[]{:S(2)}, u32[]{:S(2)}) collective-permute-start(bf16[32,128]{1,0:T(8,128)(2,1)} %get-tuple-element.19), channel_id=1, source_target_pairs={{0,2},{1,3},{2,0},{3,1},{4,6},{5,7},{6,4},{7,5},{8,10},{9,11},{10,... | collective-permute-start | bytes 24584 | tf_op jit(solution)/shard_map/ppermute | solution.py:117
  21.5 3.3 %collective-permute-start.4 = (bf16[32,128]{1,0:T(8,128)(2,1)}, bf16[32,128]{1,0:T(8,128)(2,1)S(1)}, u32[]{:S(2)}, u32[]{:S(2)}) collective-permute-start(bf16[32,128]{1,0:T(8,128)(2,1)} %get-tuple-element.20), channel_id=1, source_target_pairs={{0,3},{1,2},{2,1},{3,0},{4,7},{5,6},{6,5},{7,4},{8,11},{9,10},{10,... | collective-permute-start | bytes 24584 | tf_op jit(solution)/shard_map/ppermute | solution.py:117
  24.8 0.7 %copy-start.5 = (bf16[32,128]{1,0:T(8,128)(2,1)S(1)}, bf16[32,128]{1,0:T(8,128)(2,1)}, u32[]{:S(2)}) copy-start(bf16[32,128]{1,0:T(8,128)(2,1)} %get-tuple-element.17.refs_1_) | copy-start | bytes 24580
  25.9 1.9 %collective-permute-start.5 = (f32[1,128]{1,0:T(1,128)S(1)}, f32[1,128]{1,0:T(1,128)S(1)}, u32[]{:S(2)}, u32[]{:S(2)}) collective-permute-start(f32[1,128]{1,0:T(1,128)S(1)} %get-tuple-element.22), channel_id=1, source_target_pairs={{0,1},{1,0},{2,3},{3,2},{4,5},{5,4},{6,7},{7,6},{8,9},{9,8},{10,11... | collective-permute-start | bytes 1544 | tf_op jit(solution)/shard_map/ppermute | solution.py:117
  26.1 3.5 %collective-permute-start.6 = (f32[1,128]{1,0:T(1,128)S(1)}, f32[1,128]{1,0:T(1,128)S(1)}, u32[]{:S(2)}, u32[]{:S(2)}) collective-permute-start(f32[1,128]{1,0:T(1,128)S(1)} %get-tuple-element.23), channel_id=1, source_target_pairs={{0,2},{1,3},{2,0},{3,1},{4,6},{5,7},{6,4},{7,5},{8,10},{9,11},{10,... | collective-permute-start | bytes 1544 | tf_op jit(solution)/shard_map/ppermute | solution.py:117
  26.6 3.1 %collective-permute-start.7 = (f32[1,128]{1,0:T(1,128)S(1)}, f32[1,128]{1,0:T(1,128)S(1)}, u32[]{:S(2)}, u32[]{:S(2)}) collective-permute-start(f32[1,128]{1,0:T(1,128)S(1)} %get-tuple-element.24), channel_id=1, source_target_pairs={{0,3},{1,2},{2,1},{3,0},{4,7},{5,6},{6,5},{7,4},{8,11},{9,10},{10,... | collective-permute-start | bytes 1544 | tf_op jit(solution)/shard_map/ppermute | solution.py:117

commit v2 on v1

--- a/solution.py
+++ b/solution.py
@@ -7,10 +7,11 @@
 from jax.experimental.pallas import tpu as pltpu
 from jax.sharding import PartitionSpec as P
 
-LANES = 128
 PIECES = 4
 VMEM_SPEC = pl.BlockSpec(memory_space=pltpu.VMEM)
-ANY_SPEC = pl.BlockSpec(memory_space=pl.ANY)
+HBM_SPEC = pl.BlockSpec(memory_space=pltpu.HBM)
+SMALL = pltpu.CompilerParams(vmem_limit_bytes=4 * 2**20)
+LARGE = pltpu.CompilerParams(vmem_limit_bytes=16 * 2**20)
 
 
 def dot_nt(rows, weight):
@@ -54,13 +55,14 @@
 
 def outer_product(acts, grads, proj_in, proj_out):
     k_in, k_out = proj_in.shape[0], proj_out.shape[0]
+    args = [pltpu.with_memory_space_constraint(a, pltpu.HBM) for a in (acts, grads, proj_in, proj_out)]
     return pl.pallas_call(
         outer_kernel,
         out_shape=(
             jax.ShapeDtypeStruct((k_out, k_in), jnp.bfloat16),
             jax.ShapeDtypeStruct((k_out, k_in), jnp.float32),
         ),
-        in_specs=[ANY_SPEC] * 4,
+        in_specs=[HBM_SPEC] * 4,
         out_specs=(VMEM_SPEC, VMEM_SPEC),
         scratch_shapes=[
             pltpu.VMEM(acts.shape, jnp.bfloat16),
@@ -69,16 +71,16 @@
             pltpu.VMEM(proj_out.shape, jnp.bfloat16),
             pltpu.SemaphoreType.DMA((2 + 2 * PIECES,)),
         ],
-        compiler_params=pltpu.CompilerParams(vmem_limit_bytes=16 * 2**20),
-    )(acts, grads, proj_in, proj_out)
+        compiler_params=LARGE,
+    )(*args)
 
 
 def spread_kernel(count, own, got, *outs):
-    me = lax.axis_index("ex")
+    place = lax.axis_index("ex") // 2
     rows = own.shape[0] // count
-    for m in range(count):
-        block = pl.ds(pl.multiple_of((me ^ m) * rows, rows), rows)
-        outs[m][...] = (own[block, :] + got[block, :].astype(jnp.float32)).astype(jnp.bfloat16)
+    for k in range(count):
+        block = pl.ds(pl.multiple_of((place ^ k) * rows, rows), rows)
+        outs[k][...] = (own[block, :] + got[block, :].astype(jnp.float32)).astype(jnp.bfloat16)
 
 
 def spread(own, got, count):
@@ -88,53 +90,75 @@
         out_shape=[jax.ShapeDtypeStruct((rows, own.shape[1]), jnp.bfloat16)] * count,
         in_specs=[VMEM_SPEC] * 2,
         out_specs=[VMEM_SPEC] * count,
+        compiler_params=SMALL,
     )(own, got)
 
 
-def score_kernel(count, queries, *refs):
+def score_kernel(count, own, other, *refs):
     feats, outs = refs[:count], refs[count:]
-    table = jnp.stack([f[...].astype(jnp.float32) for f in feats], axis=0)
-    table = jnp.swapaxes(table, 0, 1)
-    table = jnp.concatenate([table[a] for a in range(table.shape[0])], axis=1)
-    raw = dot_nt(table.astype(jnp.bfloat16), queries[...])
+    core = lax.axis_index("ex") % 2
+    rows = feats[0].shape[0] // 2
+    raw = None
+    for side, queries in ((core, own), (1 - core, other)):
+        part = pl.ds(pl.multiple_of(side * rows, rows), rows)
+        table = jnp.stack([f[part, :].astype(jnp.float32) for f in feats], axis=0)
+        table = jnp.swapaxes(table, 0, 1)
+        table = jnp.concatenate([table[a] for a in range(rows)], axis=1)
+        product = dot_nt(table.astype(jnp.bfloat16), queries[...])
+        raw = product if raw is None else raw + product
     for m in range(count):
         outs[m][...] = raw[m:m + 1]
 
 
-def score(queries, feats):
+def score(own, other, feats):
     count = len(feats)
     return pl.pallas_call(
         lambda *refs: score_kernel(count, *refs),
-        out_shape=[jax.ShapeDtypeStruct((1, queries.shape[0]), jnp.float32)] * count,
-        in_specs=[VMEM_SPEC] * (count + 1),
+        out_shape=[jax.ShapeDtypeStruct((1, own.shape[0]), jnp.float32)] * count,
+        in_specs=[VMEM_SPEC] * (count + 2),
         out_specs=[VMEM_SPEC] * count,
-        compiler_params=pltpu.CompilerParams(vmem_limit_bytes=16 * 2**20),
-    )(queries, *feats)
+        compiler_params=LARGE,
+    )(own, other, *feats)
 
 
-def swap(value, axis, bit):
+def swap(value, axis, bits):
     size = lax.axis_size(axis)
-    return lax.ppermute(value, axis, [(s, s ^ bit) for s in range(size)])
+    return lax.ppermute(value, axis, [(s, s ^ bits) for s in range(size)])
+
+
+def doublings(size, start=1):
+    bits = []
+    while start < size:
+        bits.append(start)
+        start *= 2
+    return bits
 
 
 def on_device(acts, grads, proj_in, proj_out, queries):
-    layers, count = lax.axis_size("layer"), lax.axis_size("ex")
+    layers, examples = lax.axis_size("layer"), lax.axis_size("ex")
     tokens = acts.shape[2]
     low, full = outer_product(acts[0, 0], grads[0, 0], proj_in[0], proj_out[0])
-    bit = 1
-    while bit * 2 < layers:
+    *first, last = doublings(layers)
+    for bit in first:
         full = full + swap(low, "layer", bit).astype(jnp.float32)
         low = full.astype(jnp.bfloat16)
-        bit *= 2
-    blocks = spread(full, swap(low, "layer", bit), count)
-    order = sorted(range(1, count), reverse=True)
-    got = {m: swap(blocks[m], "ex", m) for m in order}
-    parts = score(queries, [blocks[0]] + [got[m] for m in range(1, count)])
-    back = {m: swap(parts[m], "ex", m) for m in order}
-    raw = parts[0]
-    for m in range(1, count):
-        raw = raw + back[m]
-    return raw * (1.0 / math.sqrt(tokens * layers))
+    other = swap(queries, "ex", 1)
+    blocks = spread(full, swap(low, "layer", last), examples // 2)
+
+    slots = {0: blocks}
+    for bit in reversed(doublings(examples, 2)):
+        half = bit // 2
+        kept = {}
+        for m, held in slots.items():
+            kept[m] = held[:half]
+            kept[m ^ bit ^ 1] = [swap(b, "ex", bit | 1) for b in held[half:]]
+        slots = kept
+    names = sorted(slots)
+    parts = dict(zip(names, score(queries, other, [slots[m][0] for m in names])))
+    for bit in reversed(doublings(examples, 2)):
+        back = {m ^ bit ^ 1: swap(parts[m], "ex", bit | 1) for m in parts if m & bit}
+        parts = {m: parts[m] + back[m] for m in parts if not m & bit}
+    return parts[0] * (1.0 / math.sqrt(tokens * layers))
 
 
 def solution(mesh):

time: 30.5 us -> 20.7 us (0.68)
  local copies, waits for them, and re-layouts: 6.11 us -> 0.01 us
  starting transfers between devices: 9.97 us -> 6.12 us
  waiting for transfers between devices: 8.83 us -> 10.1 us
  other arithmetic: 1.16 us -> 0.53 us
  Pallas kernels: 4.08 us -> 3.75 us
    unnamed x14 -> x2, local copies, waits for them, and re-layouts: 6.11 us -> 0.01 us
    ppermute x8 -> x5, starting transfers between devices: 9.97 us -> 6.12 us  [swap(): return lax.ppermute(value, axis, [(s, s ^ bits) for s in range(size)])]
    pallas_call x1, Pallas kernels: 1.45 us -> 0.01 us  [spread(): pl.pallas_call(lambda *refs: spread_kernel(count, *refs), out_shape=[jax....]
    ppermute x8 -> x5, waiting for transfers between devices: 8.83 us -> 10.1 us  [swap(): return lax.ppermute(value, axis, [(s, s ^ bits) for s in range(size)])]
    pallas_call x1, Pallas kernels: 2.25 us -> 3.1 us  [outer_product(): pl.pallas_call(outer_kernel, out_shape=(jax.ShapeDtypeStruct((k_out, k_in...]
    convert_element_type x1, other arithmetic: 0.65 us -> 0.01 us  [on_device(): low = full.astype(jnp.bfloat16)]
  transfers between devices with their start and end apart: 8 -> 5, of which waited for: 5 -> 4; matrix products, arithmetic and copies ran while one was open for 0% -> 0% of each run, Pallas kernels for 0% -> 15%
where the time goes in v2:
time: 20.7 us; the launch traced here: 20.6 us
  waiting for transfers between devices  10.1 us (49%)
  starting transfers between devices  6.12 us (30%)
  Pallas kernels  3.75 us (18%)
  other arithmetic  0.53 us (3%)
    ppermute x5, waiting for transfers between devices, swap(): return lax.ppermute(value, axis, [(s, s ^ bits) for s in range(size)])  10.1 us
    ppermute x5, starting transfers between devices, swap(): return lax.ppermute(value, axis, [(s, s ^ bits) for s in range(size)])  6.12 us
    pallas_call x1, Pallas kernels, outer_product(): pl.pallas_call(outer_kernel, out_shape=(jax.ShapeDtypeStruct((k_out, k_in...  3.1 us
    pallas_call x1, Pallas kernels, score(): pl.pallas_call(lambda *refs: score_kernel(count, *refs), out_shape=[jax.S...  0.64 us
    mul x1, other arithmetic, on_device(): return parts[0] * (1.0 / math.sqrt(tokens * layers))  0.51 us
  transfers between devices with their start and end apart: 5, of which 4 were waited for; matrix products, arithmetic and copies ran while one was open for 0% of the time, Pallas kernels for 15%

profile of v2, /device:TPU:0, one launch (start us, length us, event | category | flops | bytes accessed | tf_op | source)
XLA Modules:
  0.0 20.6 jit_solution(8248982655761557274)
XLA Ops:
  0.0 0.5 %collective-permute-start = (bf16[128,4096]{1,0:T(8,128)(2,1)}, bf16[128,4096]{1,0:T(8,128)(2,1)S(1)}, u32[]{:S(2)}, u32[]{:S(2)}) collective-permute-start(bf16[128,4096]{1,0:T(8,128)(2,1)} %refs_0_.1), channel_id=1, source_target_pairs={{0,1},{1,0},{2,3},{3,2},{4,5},{5,4},{6,7},{7,6},{8,9},{9,8},{10,11... | collective-permute-start | bytes 3145736 | tf_op jit(solution)/shard_map/ppermute | solution.py:126
  0.5 0.0 copy-start
  0.5 3.1 %shard_map.55 = (bf16[128,128]{1,0:T(8,128)(2,1)S(1)}, f32[128,128]{1,0:T(8,128)S(1)}) custom-call(bf16[256,4096]{1,0:T(8,128)(2,1)} %bitcast.4, bf16[256,1024]{1,0:T(8,128)(2,1)} %bitcast.6, bf16[128,4096]{1,0:T(8,128)(2,1)} %bitcast.5, bf16[128,1024]{1,0:T(8,128)(2,1)} %bitcast.7), custom_call_target="tpu_custom_call" | custom-call | tf_op jit(solution)/shard_map/pallas_call | solution.py:59
  3.6 2.6 %collective-permute-start.1 = (bf16[128,128]{1,0:T(8,128)(2,1)S(1)}, bf16[128,128]{1,0:T(8,128)(2,1)S(1)}, u32[]{:S(2)}, u32[]{:S(2)}) collective-permute-start(bf16[128,128]{1,0:T(8,128)(2,1)S(1)} %get-tuple-element.12), channel_id=1, source_target_pairs={{0,4},{4,0},{8,12},{12,8},{1,5},{5,1},{9,13},{13,9},{2,6},{6,2},{1... | collective-permute-start | bytes 98312 | tf_op jit(solution)/shard_map/ppermute | solution.py:126
  6.2 2.1 %collective-permute-done.1 = bf16[128,128]{1,0:T(8,128)(2,1)S(1)} collective-permute-done((bf16[128,128]{1,0:T(8,128)(2,1)S(1)}, bf16[128,128]{1,0:T(8,128)(2,1)S(1)}, u32[]{:S(2)}, u32[]{:S(2)}) %collective-permute-start.1) | collective-permute-done | bytes 32800 | tf_op jit(solution)/shard_map/ppermute | solution.py:126
  8.3 2.9 %collective-permute-start.2 = (bf16[128,128]{1,0:T(8,128)(2,1)S(1)}, bf16[128,128]{1,0:T(8,128)(2,1)S(1)}, u32[]{:S(2)}, u32[]{:S(2)}) collective-permute-start(bf16[128,128]{1,0:T(8,128)(2,1)S(1)} %get-tuple-element.17), channel_id=1, source_target_pairs={{0,8},{4,12},{8,0},{12,4},{1,9},{5,13},{9,1},{13,5},{2,10},{6,14},... | collective-permute-start | bytes 98312 | tf_op jit(solution)/shard_map/ppermute | solution.py:126
  11.2 2.0 %collective-permute-done.2.refs_1_ = bf16[128,128]{1,0:T(8,128)(2,1)S(1)} collective-permute-done((bf16[128,128]{1,0:T(8,128)(2,1)S(1)}, bf16[128,128]{1,0:T(8,128)(2,1)S(1)}, u32[]{:S(2)}, u32[]{:S(2)}) %collective-permute-start.2) | collective-permute-done | bytes 32800 | tf_op jit(solution)/shard_map/ppermute | solution.py:126
  13.2 0.1 collective-permute-start.3
  13.3 3.2 %collective-permute-done.3.refs_3_ = bf16[64,128]{1,0:T(8,128)(2,1)S(1)} collective-permute-done((bf16[64,128]{1,0:T(8,128)(2,1)S(1)}, bf16[64,128]{1,0:T(8,128)(2,1)S(1)}, u32[]{:S(2)}, u32[]{:S(2)}) %collective-permute-start.3) | collective-permute-done | bytes 16416 | tf_op jit(solution)/shard_map/ppermute | solution.py:126
  16.4 0.0 collective-permute-done.refs_1_
  16.4 0.0 copy-done
  16.4 0.6 %shard_map.57 = (f32[1,128]{1,0:T(1,128)S(1)}, f32[1,128]{1,0:T(1,128)S(1)}) custom-call(bf16[128,4096]{1,0:T(8,128)(2,1)S(1)} %copy-done, bf16[128,4096]{1,0:T(8,128)(2,1)S(1)} %collective-permute-done.refs_1_, bf16[64,128]{1,0:T(8,128)(2,1)S(1)} %get-tuple-element.13.refs_2_, bf16[64,128]{1,0:T(8,128)(2,1)S(1)} %collective-permute-done.3.refs_3_), custom_call_target="tpu_custom_call" | custom-call | tf_op jit(solution)/shard_map/pallas_call | solution.py:115
  17.1 0.0 collective-permute-start.4
  17.1 3.0 %collective-permute-done.4 = f32[1,128]{1,0:T(1,128)S(1)} collective-permute-done((f32[1,128]{1,0:T(1,128)S(1)}, f32[1,128]{1,0:T(1,128)S(1)}, u32[]{:S(2)}, u32[]{:S(2)}) %collective-permute-start.4) | collective-permute-done | bytes 544 | tf_op jit(solution)/shard_map/ppermute | solution.py:126
  20.1 0.5 %add_multiply_fusion = f32[1,128]{1,0:T(1,128)} fusion(f32[1,128]{1,0:T(1,128)S(1)} %get-tuple-element.15, f32[1,128]{1,0:T(1,128)S(1)} %collective-permute-done.4), kind=kLoop, calls=%fused_computation.1 | loop fusion | flops 256 | bytes 1536 | tf_op jit(solution)/shard_map/mul | solution.py:161
  (2 shorter events, 0.0 us)
Async XLA Ops:
  0.0 16.4 %collective-permute-start = (bf16[128,4096]{1,0:T(8,128)(2,1)}, bf16[128,4096]{1,0:T(8,128)(2,1)S(1)}, u32[]{:S(2)}, u32[]{:S(2)}) collective-permute-start(bf16[128,4096]{1,0:T(8,128)(2,1)} %refs_0_.1), channel_id=1, source_target_pairs={{0,1},{1,0},{2,3},{3,2},{4,5},{5,4},{6,7},{7,6},{8,9},{9,8},{10,11... | collective-permute-start | bytes 3145736 | tf_op jit(solution)/shard_map/ppermute | solution.py:126
  0.5 16.0 %copy-start = (bf16[128,4096]{1,0:T(8,128)(2,1)S(1)}, bf16[128,4096]{1,0:T(8,128)(2,1)}, u32[]{:S(2)}) copy-start(bf16[128,4096]{1,0:T(8,128)(2,1)} %refs_0_.1) | copy-start | bytes 3145732
  3.6 4.7 %collective-permute-start.1 = (bf16[128,128]{1,0:T(8,128)(2,1)S(1)}, bf16[128,128]{1,0:T(8,128)(2,1)S(1)}, u32[]{:S(2)}, u32[]{:S(2)}) collective-permute-start(bf16[128,128]{1,0:T(8,128)(2,1)S(1)} %get-tuple-element.12), channel_id=1, source_target_pairs={{0,4},{4,0},{8,12},{12,8},{1,5},{5,1},{9,13},{13,9},{2,6},{6,2},{1... | collective-permute-start | bytes 98312 | tf_op jit(solution)/shard_map/ppermute | solution.py:126
  8.3 4.9 %collective-permute-start.2 = (bf16[128,128]{1,0:T(8,128)(2,1)S(1)}, bf16[128,128]{1,0:T(8,128)(2,1)S(1)}, u32[]{:S(2)}, u32[]{:S(2)}) collective-permute-start(bf16[128,128]{1,0:T(8,128)(2,1)S(1)} %get-tuple-element.17), channel_id=1, source_target_pairs={{0,8},{4,12},{8,0},{12,4},{1,9},{5,13},{9,1},{13,5},{2,10},{6,14},... | collective-permute-start | bytes 98312 | tf_op jit(solution)/shard_map/ppermute | solution.py:126
  13.2 3.2 %collective-permute-start.3 = (bf16[64,128]{1,0:T(8,128)(2,1)S(1)}, bf16[64,128]{1,0:T(8,128)(2,1)S(1)}, u32[]{:S(2)}, u32[]{:S(2)}) collective-permute-start(bf16[64,128]{1,0:T(8,128)(2,1)S(1)} %get-tuple-element.14), channel_id=1, source_target_pairs={{0,3},{1,2},{2,1},{3,0},{4,7},{5,6},{6,5},{7,4},{8,11},{9,10},{10,... | collective-permute-start | bytes 49160 | tf_op jit(solution)/shard_map/ppermute | solution.py:126
  17.1 3.0 %collective-permute-start.4 = (f32[1,128]{1,0:T(1,128)S(1)}, f32[1,128]{1,0:T(1,128)S(1)}, u32[]{:S(2)}, u32[]{:S(2)}) collective-permute-start(f32[1,128]{1,0:T(1,128)S(1)} %get-tuple-element.16), channel_id=1, source_target_pairs={{0,3},{1,2},{2,1},{3,0},{4,7},{5,6},{6,5},{7,4},{8,11},{9,10},{10,... | collective-permute-start | bytes 1544 | tf_op jit(solution)/shard_map/ppermute | solution.py:126

commit v3 on v2

v3 whole, which is shorter than its diff:
```python
import math

import jax
import jax.numpy as jnp
from jax import lax
from jax.experimental import pallas as pl
from jax.experimental.pallas import tpu as pltpu
from jax.sharding import PartitionSpec as P

VMEM_SPEC = pl.BlockSpec(memory_space=pltpu.VMEM)
SMALL = pltpu.CompilerParams(vmem_limit_bytes=4 * 2**20)
LARGE = pltpu.CompilerParams(vmem_limit_bytes=16 * 2**20)


def dot_nt(rows, weight):
    return lax.dot_general(
        rows, weight, (((1,), (1,)), ((), ())), preferred_element_type=jnp.float32
    )


def outer_kernel(x_low, grads, proj_out, low_ref, full_ref):
    g_low = dot_nt(proj_out[...], grads[...]).astype(jnp.bfloat16)
    outer = jnp.dot(g_low, x_low[...], preferred_element_type=jnp.float32)
    full_ref[...] = outer
    low_ref[...] = outer.astype(jnp.bfloat16)


def outer_product(x_low, grads, proj_out):
    shape = (proj_out.shape[0], x_low.shape[1])
    return pl.pallas_call(
        outer_kernel,
        out_shape=(jax.ShapeDtypeStruct(shape, jnp.bfloat16), jax.ShapeDtypeStruct(shape, jnp.float32)),
        in_specs=[VMEM_SPEC] * 3,
        out_specs=(VMEM_SPEC, VMEM_SPEC),
        compiler_params=SMALL,
        name="outer_product",
    )(x_low, grads, proj_out)


def spread_kernel(count, own, got, *outs):
    place = lax.axis_index("ex") // 2
    rows = own.shape[0] // count
    for k in range(count):
        block = pl.ds(pl.multiple_of((place ^ k) * rows, rows), rows)
        outs[k][...] = (own[block, :] + got[block, :].astype(jnp.float32)).astype(jnp.bfloat16)


def spread(own, got, count):
    rows = own.shape[0] // count
    return pl.pallas_call(
        lambda *refs: spread_kernel(count, *refs),
        out_shape=[jax.ShapeDtypeStruct((rows, own.shape[1]), jnp.bfloat16)] * count,
        in_specs=[VMEM_SPEC] * 2,
        out_specs=[VMEM_SPEC] * count,
        compiler_params=SMALL,
        name="spread",
    )(own, got)


def turn_kernel(own, other, out):
    width = own.shape[1]
    out[:width, :] = own[...].T
    out[width:, :] = other[...].T


def turn(own, other):
    return pl.pallas_call(
        turn_kernel,
        out_shape=jax.ShapeDtypeStruct((2 * own.shape[1], own.shape[0]), own.dtype),
        in_specs=[VMEM_SPEC] * 2,
        out_specs=VMEM_SPEC,
        compiler_params=LARGE,
        name="turn",
    )(own, other)


def score_kernel(count, queries, *refs):
    feats, outs = refs[: 2 * count], refs[2 * count:]
    core = lax.axis_index("ex") % 2
    rows = feats[0].shape[0] // 2
    width = queries.shape[0] // 2
    raw = None
    for side, half in ((core, 0), (1 - core, 1)):
        part = pl.ds(pl.multiple_of(side * rows, rows), rows)
        table = jnp.stack(
            [feats[2 * m][part, :].astype(jnp.float32) + feats[2 * m + 1][part, :].astype(jnp.float32)
             for m in range(count)], axis=0)
        table = jnp.swapaxes(table, 0, 1)
        table = jnp.concatenate([table[a] for a in range(rows)], axis=1)
        product = jnp.dot(
            table.astype(jnp.bfloat16), queries[half * width:(half + 1) * width, :],
            preferred_element_type=jnp.float32)
        raw = product if raw is None else raw + product
    for m in range(count):
        outs[m][...] = raw[m:m + 1]


def score(queries, feats):
    count = len(feats)
    return pl.pallas_call(
        lambda *refs: score_kernel(count, *refs),
        out_shape=[jax.ShapeDtypeStruct((1, queries.shape[1]), jnp.float32)] * count,
        in_specs=[VMEM_SPEC] * (2 * count + 1),
        out_specs=[VMEM_SPEC] * count,
        compiler_params=LARGE,
        name="score",
    )(queries, *[f for pair in feats for f in pair])


def swap(value, layer_bits, ex_bits):
    layers, examples = lax.axis_size("layer"), lax.axis_size("ex")
    pairs = [
        (l * examples + e, (l ^ layer_bits) * examples + (e ^ ex_bits))
        for l in range(layers) for e in range(examples)
    ]
    return lax.ppermute(value, ("layer", "ex"), pairs)


def doublings(size, start=1):
    bits = []
    while start < size:
        bits.append(start)
        start *= 2
    return bits


ORDER = (0, 1, 2)


def on_device(acts, grads, proj_in, proj_out, queries):
    layers, examples = lax.axis_size("layer"), lax.axis_size("ex")
    tokens = acts.shape[2]
    x_low = dot_nt(acts[0, 0], proj_in[0]).astype(jnp.bfloat16)
    low, full = outer_product(x_low, grads[0, 0], proj_out[0])
    joint, *first, last = doublings(layers)
    for bit in first:
        full = full + swap(low, bit, 0).astype(jnp.float32)
        low = full.astype(jnp.bfloat16)
    low, queries = lax.optimization_barrier((low, queries))
    got = swap(low, last, 0)
    other = swap(queries, 0, 1)
    blocks = spread(full, got, examples // 2)

    slots = {0: blocks}
    *outer, inner = reversed(doublings(examples, 2))
    for bit in outer:
        half = bit // 2
        kept = {}
        for m, held in slots.items():
            kept[m] = held[:half]
            kept[m ^ bit ^ 1] = [swap(b, 0, bit | 1) for b in held[half:]]
        slots = kept
    pairs = {}
    for m, (keep, give) in slots.items():
        come = {}
        for step in ORDER:
            if step == 0:
                come[0] = swap(give, 0, inner | 1)
            elif step == 1:
                come[1] = swap(keep, joint, 0)
            else:
                come[2] = swap(give, joint, inner | 1)
        pairs[m] = (keep, come[1])
        pairs[m ^ inner ^ 1] = (come[0], come[2])
    names = sorted(pairs)
    table = turn(queries, other)
    parts = dict(zip(names, score(table, [pairs[m] for m in names])))
    for bit in reversed(doublings(examples, 2)):
        back = {m ^ bit ^ 1: swap(parts[m], 0, bit | 1) for m in parts if m & bit}
        parts = {m: parts[m] + back[m] for m in parts if not m & bit}
    return parts[0] * (1.0 / math.sqrt(tokens * layers))


def solution(mesh):
    placed = (
        P("layer", ("groups", "ex"), None, None),
        P("layer", ("groups", "ex"), None, None),
        P("layer", None, None),
        P("layer", None, None),
        P("layer", "ex"),
    )
    return jax.shard_map(
        on_device,
        mesh=mesh,
        in_specs=placed,
        out_specs=P(("groups", "ex"), "layer"),
        check_vma=False,
    )
```

time: 20.7 us -> 20.4 us (0.986)
  waiting for transfers between devices: 10.1 us -> 6.23 us
  Pallas kernels: 3.75 us -> 1.4 us
  starting transfers between devices: 6.12 us -> 8.3 us
  matrix products: 0 us -> 2.01 us
  local copies, waits for them, and re-layouts: 0.01 us -> 1.6 us
    ppermute x5 -> x6, waiting for transfers between devices: 10.1 us -> 6.23 us  [swap(): return lax.ppermute(value, ('layer', 'ex'), pairs)]
    ppermute x5 -> x6, starting transfers between devices: 6.12 us -> 8.3 us  [swap(): return lax.ppermute(value, ('layer', 'ex'), pairs)]
    pallas_call x1 -> x2, Pallas kernels: 3.1 us -> 1.01 us  [the longest x1 0.59 us: turn(): pl.pallas_call(turn_kernel, out_shape=jax.ShapeDtypeStruct((2 * own.shape...]
    dot_general x0 -> x1, matrix products: none -> 2.01 us  [dot_nt(): lax.dot_general(rows, weight, (((1,), (1,)), ((), ())), preferred_element...]
    unnamed x2 -> x8, local copies, waits for them, and re-layouts: 0.01 us -> 1.6 us
    pallas_call x1, Pallas kernels: 0.64 us -> 0.38 us  [score(): pl.pallas_call(lambda *refs: score_kernel(count, *refs), out_shape=[jax.S...]
  transfers between devices with their start and end apart: 5 -> 6, of which waited for: 4 -> 3; matrix products, arithmetic and copies ran while one was open for 0% -> 0% of each run, Pallas kernels for 15% -> 3%
where the time goes in v3:
time: 20.4 us; the launch traced here: 20.1 us
  starting transfers between devices  8.3 us (41%)
  waiting for transfers between devices  6.23 us (31%)
  matrix products  2.01 us (10%)
  local copies, waits for them, and re-layouts  1.6 us (8%)
  Pallas kernels  1.4 us (7%)
  other arithmetic  0.51 us (2%)
    ppermute x6, starting transfers between devices, swap(): return lax.ppermute(value, ('layer', 'ex'), pairs)  8.3 us
    ppermute x6, waiting for transfers between devices, swap(): return lax.ppermute(value, ('layer', 'ex'), pairs)  6.23 us
    dot_general x1, matrix products, dot_nt(): lax.dot_general(rows, weight, (((1,), (1,)), ((), ())), preferred_element...  2.01 us
    unnamed x8, local copies, waits for them, and re-layouts  1.6 us
    pallas_call x1, Pallas kernels, turn(): pl.pallas_call(turn_kernel, out_shape=jax.ShapeDtypeStruct((2 * own.shape...  0.59 us
    mul x1, other arithmetic, on_device(): return parts[0] * (1.0 / math.sqrt(tokens * layers))  0.51 us
    pallas_call x1, Pallas kernels, outer_product(): pl.pallas_call(outer_kernel, out_shape=(jax.ShapeDtypeStruct(shape, jnp.b...  0.42 us
  transfers between devices with their start and end apart: 6, of which 3 were waited for; matrix products, arithmetic and copies ran while one was open for 0% of the time, Pallas kernels for 3%

profile of v3, /device:TPU:0, one launch (start us, length us, event | category | flops | bytes accessed | tf_op | source)
XLA Modules:
  0.0 20.1 jit_solution(12245726360907737222)
XLA Ops:
  0.0 0.0 copy-start
  0.0 0.0 copy-start.3
  0.0 0.0 copy-start.2
  0.0 1.6 %copy-done = bf16[1,1,256,4096]{3,2,1,0:T(8,128)(2,1)S(1)} copy-done((bf16[1,1,256,4096]{3,2,1,0:T(8,128)(2,1)S(1)}, bf16[1,1,256,4096]{3,2,1,0:T(8,128)(2,1)}, u32[]{:S(2)}) %copy-start) | copy-done | bytes 2097176
  1.6 0.0 copy-start.1
  1.6 2.0 %fusion.2.x_low = bf16[256,128]{1,0:T(8,128)(2,1)S(1)} fusion(bf16[1,1,256,4096]{3,2,1,0:T(8,128)(2,1)S(1)} %copy-done, bf16[1,128,4096]{2,1,0:T(8,128)(2,1)} %param.7), kind=kOutput, calls=%fused_computation.2 | convolution fusion | flops 268468224 | bytes 3211264 | tf_op jit(solution)/shard_map/dot_general | solution.py:16
  3.6 0.0 copy-done.3
  3.6 0.0 copy-done.2
  3.6 0.4 %outer_product.1 = (bf16[128,128]{1,0:T(8,128)(2,1)S(1)}, f32[128,128]{1,0:T(8,128)S(1)}) custom-call(bf16[256,128]{1,0:T(8,128)(2,1)S(1)} %fusion.2.x_low, bf16[256,1024]{1,0:T(8,128)(2,1)S(1)} %bitcast.10, bf16[128,1024]{1,0:T(8,128)(2,1)S(1)} %bitcast.11), custom_call_target="tpu_custom_call" | custom-call | tf_op jit(solution)/shard_map/outer_product/pallas_call | solution.py:30
  4.1 0.0 copy-done.1
  4.1 0.5 %collective-permute-start = (bf16[128,4096]{1,0:T(8,128)(2,1)S(1)}, bf16[128,4096]{1,0:T(8,128)(2,1)S(1)}, u32[]{:S(2)}, u32[]{:S(2)}) collective-permute-start(bf16[128,4096]{1,0:T(8,128)(2,1)S(1)} %copy-done.1), channel_id=1, source_target_pairs={{0,1},{1,0},{2,3},{3,2},{4,5},{5,4},{6,7},{7,6},{8,9},{9,8},{10,11... | collective-permute-start | bytes 3145736 | tf_op jit(solution)/shard_map/ppermute | solution.py:116
  4.6 3.7 %collective-permute-start.1 = (bf16[128,128]{1,0:T(8,128)(2,1)S(1)}, bf16[128,128]{1,0:T(8,128)(2,1)S(1)}, u32[]{:S(2)}, u32[]{:S(2)}) collective-permute-start(bf16[128,128]{1,0:T(8,128)(2,1)S(1)} %get-tuple-element.16), channel_id=1, source_target_pairs={{0,8},{1,9},{2,10},{3,11},{4,12},{5,13},{6,14},{7,15},{8,0},{9,1},... | collective-permute-start | bytes 98312 | tf_op jit(solution)/shard_map/ppermute | solution.py:116
  8.3 2.0 %collective-permute-done.1.refs_1_ = bf16[128,128]{1,0:T(8,128)(2,1)S(1)} collective-permute-done((bf16[128,128]{1,0:T(8,128)(2,1)S(1)}, bf16[128,128]{1,0:T(8,128)(2,1)S(1)}, u32[]{:S(2)}, u32[]{:S(2)}) %collective-permute-start.1) | collective-permute-done | bytes 32800 | tf_op jit(solution)/shard_map/ppermute | solution.py:116
  10.3 1.9 %collective-permute-start.2 = (bf16[64,128]{1,0:T(8,128)(2,1)S(1)}, bf16[64,128]{1,0:T(8,128)(2,1)S(1)}, u32[]{:S(2)}, u32[]{:S(2)}) collective-permute-start(bf16[64,128]{1,0:T(8,128)(2,1)S(1)} %get-tuple-element.17.refs_1_), channel_id=1, source_target_pairs={{0,4},{1,5},{2,6},{3,7},{4,0},{5,1},{6,2},{7,3},{8,12},{9,13},{10,... | collective-permute-start | bytes 49160 | tf_op jit(solution)/shard_map/ppermute | solution.py:116
  12.1 0.0 collective-permute-start.4
  12.1 1.4 %collective-permute-start.3 = (bf16[64,128]{1,0:T(8,128)(2,1)S(1)}, bf16[64,128]{1,0:T(8,128)(2,1)S(1)}, u32[]{:S(2)}, u32[]{:S(2)}) collective-permute-start(bf16[64,128]{1,0:T(8,128)(2,1)S(1)} %get-tuple-element.18), channel_id=1, source_target_pairs={{0,3},{1,2},{2,1},{3,0},{4,7},{5,6},{6,5},{7,4},{8,11},{9,10},{10,... | collective-permute-start | bytes 49160 | tf_op jit(solution)/shard_map/ppermute | solution.py:116
  13.5 0.0 collective-permute-done.other
  13.5 0.6 %turn.1.refs_0_ = bf16[8192,128]{1,0:T(8,128)(2,1)S(1)} custom-call(bf16[128,4096]{1,0:T(8,128)(2,1)S(1)} %copy-done.1, bf16[128,4096]{1,0:T(8,128)(2,1)S(1)} %collective-permute-done.other), custom_call_target="tpu_custom_call" | custom-call | tf_op jit(solution)/shard_map/turn/pallas_call | solution.py:67
  14.1 0.0 collective-permute-done.2.refs_2_
  14.1 2.1 %collective-permute-done.4.refs_4_ = bf16[64,128]{1,0:T(8,128)(2,1)S(1)} collective-permute-done((bf16[64,128]{1,0:T(8,128)(2,1)S(1)}, bf16[64,128]{1,0:T(8,128)(2,1)S(1)}, u32[]{:S(2)}, u32[]{:S(2)}) %collective-permute-start.4) | collective-permute-done | bytes 16416 | tf_op jit(solution)/shard_map/ppermute | solution.py:116
  16.2 0.0 collective-permute-done.3.refs_3_
  16.2 0.4 %score.1 = (f32[1,128]{1,0:T(1,128)S(1)}, f32[1,128]{1,0:T(1,128)S(1)}) custom-call(bf16[8192,128]{1,0:T(8,128)(2,1)S(1)} %turn.1.refs_0_, bf16[64,128]{1,0:T(8,128)(2,1)S(1)} %get-tuple-element.17.refs_1_, bf16[64,128]{1,0:T(8,128)(2,1)S(1)} %collective-permute-done.2.refs_2_, bf16[64,128]{1,0:T(8,128)(2,1)S(1)} %collective-permute-done.3.refs_3_, ...), custom_call_target="tpu_custom_call" | custom-call | tf_op jit(solution)/shard_map/score/pallas_call | solution.py:100
  16.6 0.8 %collective-permute-start.5 = (f32[1,128]{1,0:T(1,128)S(1)}, f32[1,128]{1,0:T(1,128)S(1)}, u32[]{:S(2)}, u32[]{:S(2)}) collective-permute-start(f32[1,128]{1,0:T(1,128)S(1)} %get-tuple-element.20), channel_id=1, source_target_pairs={{0,3},{1,2},{2,1},{3,0},{4,7},{5,6},{6,5},{7,4},{8,11},{9,10},{10,... | collective-permute-start | bytes 1544 | tf_op jit(solution)/shard_map/ppermute | solution.py:116
  17.4 2.2 %collective-permute-done.5 = f32[1,128]{1,0:T(1,128)S(1)} collective-permute-done((f32[1,128]{1,0:T(1,128)S(1)}, f32[1,128]{1,0:T(1,128)S(1)}, u32[]{:S(2)}, u32[]{:S(2)}) %collective-permute-start.5) | collective-permute-done | bytes 544 | tf_op jit(solution)/shard_map/ppermute | solution.py:116
  19.6 0.5 %add_multiply_fusion = f32[1,128]{1,0:T(1,128)} fusion(f32[1,128]{1,0:T(1,128)S(1)} %get-tuple-element.19, f32[1,128]{1,0:T(1,128)S(1)} %collective-permute-done.5), kind=kLoop, calls=%fused_computation.4 | loop fusion | flops 256 | bytes 1536 | tf_op jit(solution)/shard_map/mul | solution.py:171
  (1 shorter events, 0.0 us)
Async XLA Ops:
  0.0 1.6 %copy-start = (bf16[1,1,256,4096]{3,2,1,0:T(8,128)(2,1)S(1)}, bf16[1,1,256,4096]{3,2,1,0:T(8,128)(2,1)}, u32[]{:S(2)}) copy-start(bf16[1,1,256,4096]{3,2,1,0:T(8,128)(2,1)} %param.5) | copy-start | bytes 6291460
  0.0 3.6 %copy-start.3 = (bf16[1,128,1024]{2,1,0:T(8,128)(2,1)S(1)}, bf16[1,128,1024]{2,1,0:T(8,128)(2,1)}, u32[]{:S(2)}) copy-start(bf16[1,128,1024]{2,1,0:T(8,128)(2,1)} %param.8) | copy-start | bytes 786436
  0.0 3.6 %copy-start.2 = (bf16[1,1,256,1024]{3,2,1,0:T(8,128)(2,1)S(1)}, bf16[1,1,256,1024]{3,2,1,0:T(8,128)(2,1)}, u32[]{:S(2)}) copy-start(bf16[1,1,256,1024]{3,2,1,0:T(8,128)(2,1)} %param.6) | copy-start | bytes 1572868
  1.6 2.5 %copy-start.1 = (bf16[128,4096]{1,0:T(8,128)(2,1)S(1)}, bf16[128,4096]{1,0:T(8,128)(2,1)}, u32[]{:S(2)}) copy-start(bf16[128,4096]{1,0:T(8,128)(2,1)} %own) | copy-start | bytes 3145732
  4.1 9.5 %collective-permute-start = (bf16[128,4096]{1,0:T(8,128)(2,1)S(1)}, bf16[128,4096]{1,0:T(8,128)(2,1)S(1)}, u32[]{:S(2)}, u32[]{:S(2)}) collective-permute-start(bf16[128,4096]{1,0:T(8,128)(2,1)S(1)} %copy-done.1), channel_id=1, source_target_pairs={{0,1},{1,0},{2,3},{3,2},{4,5},{5,4},{6,7},{7,6},{8,9},{9,8},{10,11... | collective-permute-start | bytes 3145736 | tf_op jit(solution)/shard_map/ppermute | solution.py:116
  4.6 5.6 %collective-permute-start.1 = (bf16[128,128]{1,0:T(8,128)(2,1)S(1)}, bf16[128,128]{1,0:T(8,128)(2,1)S(1)}, u32[]{:S(2)}, u32[]{:S(2)}) collective-permute-start(bf16[128,128]{1,0:T(8,128)(2,1)S(1)} %get-tuple-element.16), channel_id=1, source_target_pairs={{0,8},{1,9},{2,10},{3,11},{4,12},{5,13},{6,14},{7,15},{8,0},{9,1},... | collective-permute-start | bytes 98312 | tf_op jit(solution)/shard_map/ppermute | solution.py:116
  10.3 3.9 %collective-permute-start.2 = (bf16[64,128]{1,0:T(8,128)(2,1)S(1)}, bf16[64,128]{1,0:T(8,128)(2,1)S(1)}, u32[]{:S(2)}, u32[]{:S(2)}) collective-permute-start(bf16[64,128]{1,0:T(8,128)(2,1)S(1)} %get-tuple-element.17.refs_1_), channel_id=1, source_target_pairs={{0,4},{1,5},{2,6},{3,7},{4,0},{5,1},{6,2},{7,3},{8,12},{9,13},{10,... | collective-permute-start | bytes 49160 | tf_op jit(solution)/shard_map/ppermute | solution.py:116
  12.1 4.1 %collective-permute-start.4 = (bf16[64,128]{1,0:T(8,128)(2,1)S(1)}, bf16[64,128]{1,0:T(8,128)(2,1)S(1)}, u32[]{:S(2)}, u32[]{:S(2)}) collective-permute-start(bf16[64,128]{1,0:T(8,128)(2,1)S(1)} %get-tuple-element.18), channel_id=1, source_target_pairs={{0,7},{1,6},{2,5},{3,4},{4,3},{5,2},{6,1},{7,0},{8,15},{9,14},{10,... | collective-permute-start | bytes 49160 | tf_op jit(solution)/shard_map/ppermute | solution.py:116
  12.1 4.1 %collective-permute-start.3 = (bf16[64,128]{1,0:T(8,128)(2,1)S(1)}, bf16[64,128]{1,0:T(8,128)(2,1)S(1)}, u32[]{:S(2)}, u32[]{:S(2)}) collective-permute-start(bf16[64,128]{1,0:T(8,128)(2,1)S(1)} %get-tuple-element.18), channel_id=1, source_target_pairs={{0,3},{1,2},{2,1},{3,0},{4,7},{5,6},{6,5},{7,4},{8,11},{9,10},{10,... | collective-permute-start | bytes 49160 | tf_op jit(solution)/shard_map/ppermute | solution.py:116
  16.6 3.0 %collective-permute-start.5 = (f32[1,128]{1,0:T(1,128)S(1)}, f32[1,128]{1,0:T(1,128)S(1)}, u32[]{:S(2)}, u32[]{:S(2)}) collective-permute-start(f32[1,128]{1,0:T(1,128)S(1)} %get-tuple-element.20), channel_id=1, source_target_pairs={{0,3},{1,2},{2,1},{3,0},{4,7},{5,6},{6,5},{7,4},{8,11},{9,10},{10,... | collective-permute-start | bytes 1544 | tf_op jit(solution)/shard_map/ppermute | solution.py:116

commit v4 on v3

v4 whole, which is shorter than its diff:
```python
import math

import jax
import jax.numpy as jnp
from jax import lax
from jax.experimental import pallas as pl
from jax.experimental.pallas import tpu as pltpu
from jax.sharding import PartitionSpec as P

PIECES = 2
VMEM_SPEC = pl.BlockSpec(memory_space=pltpu.VMEM)
HBM_SPEC = pl.BlockSpec(memory_space=pltpu.HBM)
SMALL = pltpu.CompilerParams(vmem_limit_bytes=4 * 2**20)
LARGE = pltpu.CompilerParams(vmem_limit_bytes=16 * 2**20)


def dot_nt(rows, weight):
    return lax.dot_general(
        rows, weight, (((1,), (1,)), ((), ())), preferred_element_type=jnp.float32
    )


def outer_kernel(acts, grads, proj_in, proj_out, low_ref, full_ref, a_buf, g_buf, pi_buf, po_buf, sems):
    width = acts.shape[1] // PIECES

    def piece(k):
        cols = pl.ds(k * width if isinstance(k, int) else pl.multiple_of(k * width, width), width)
        return cols, (
            pltpu.make_async_copy(proj_in.at[:, cols], pi_buf.at[:, cols], sems.at[2 + 2 * k]),
            pltpu.make_async_copy(acts.at[:, cols], a_buf.at[:, cols], sems.at[3 + 2 * k]),
        )

    out_copies = (
        pltpu.make_async_copy(proj_out, po_buf, sems.at[0]),
        pltpu.make_async_copy(grads, g_buf, sems.at[1]),
    )
    for copy in out_copies:
        copy.start()
    for k in range(PIECES):
        for copy in piece(k)[1]:
            copy.start()
    for copy in out_copies:
        copy.wait()
    g_low = dot_nt(po_buf[...], g_buf[...]).astype(jnp.bfloat16)

    def add_piece(k, total):
        cols, copies = piece(k)
        for copy in copies:
            copy.wait()
        return total + dot_nt(a_buf[:, cols], pi_buf[:, cols])

    x_low = lax.fori_loop(
        0, PIECES, add_piece, jnp.zeros((acts.shape[0], proj_in.shape[0]), jnp.float32))
    outer = jnp.dot(g_low, x_low.astype(jnp.bfloat16), preferred_element_type=jnp.float32)
    full_ref[...] = outer
    low_ref[...] = outer.astype(jnp.bfloat16)


def outer_product(*args):
    acts, grads, proj_in, proj_out = args
    shape = (proj_out.shape[0], proj_in.shape[0])
    return pl.pallas_call(
        outer_kernel,
        out_shape=(jax.ShapeDtypeStruct(shape, jnp.bfloat16), jax.ShapeDtypeStruct(shape, jnp.float32)),
        in_specs=[HBM_SPEC] * 4,
        out_specs=(VMEM_SPEC, VMEM_SPEC),
        scratch_shapes=[pltpu.VMEM(a.shape, a.dtype) for a in args]
        + [pltpu.SemaphoreType.DMA((2 + 2 * PIECES,))],
        compiler_params=LARGE,
        name="outer_product",
    )(*[pltpu.with_memory_space_constraint(a, pltpu.HBM) for a in args])


def spread_kernel(count, own, got, *outs):
    place = lax.axis_index("ex") // 2
    rows = own.shape[0] // count
    for k in range(count):
        block = pl.ds(pl.multiple_of((place ^ k) * rows, rows), rows)
        total = (own[block, :] + got[block, :].astype(jnp.float32)).astype(jnp.bfloat16)
        outs[k][...] = total
        outs[k + count][...] = total


def spread(own, got, count):
    rows = own.shape[0] // count
    outs = pl.pallas_call(
        lambda *refs: spread_kernel(count, *refs),
        out_shape=[jax.ShapeDtypeStruct((rows, own.shape[1]), jnp.bfloat16)] * (2 * count),
        in_specs=[VMEM_SPEC] * 2,
        out_specs=[VMEM_SPEC] * (2 * count),
        compiler_params=SMALL,
        name="spread",
    )(own, got)
    return list(zip(outs[:count], outs[count:]))


def turn_kernel(own, other, out):
    width = own.shape[1]
    out[:width, :] = own[...].T
    out[width:, :] = other[...].T


def turn(own, other):
    return pl.pallas_call(
        turn_kernel,
        out_shape=jax.ShapeDtypeStruct((2 * own.shape[1], own.shape[0]), own.dtype),
        in_specs=[VMEM_SPEC] * 2,
        out_specs=VMEM_SPEC,
        compiler_params=LARGE,
        name="turn",
    )(own, other)


def score_kernel(count, queries, *refs):
    near, far, outs = refs[:count], refs[count:2 * count], refs[2 * count:]
    core = lax.axis_index("ex") % 2
    rows = near[0].shape[0] // 2
    width = queries.shape[0] // 2
    raw = None
    for side, half in ((core, 0), (1 - core, 1)):
        part = pl.ds(pl.multiple_of(side * rows, rows), rows)
        table = jnp.stack(
            [a[part, :].astype(jnp.float32) + b[part, :].astype(jnp.float32) for a, b in zip(near, far)], axis=0)
        table = jnp.swapaxes(table, 0, 1)
        table = jnp.concatenate([table[a] for a in range(rows)], axis=1)
        product = jnp.dot(
            table.astype(jnp.bfloat16), queries[half * width:(half + 1) * width, :],
            preferred_element_type=jnp.float32)
        raw = product if raw is None else raw + product
    for m in range(count):
        outs[m][...] = raw[m:m + 1]


def score(queries, near, far):
    count = len(near)

    def kernel(queries, *refs):
        half = count // 2
        parts = [refs[k * half:(k + 1) * half] for k in range(4)]
        score_kernel(count, queries, *parts[0], *parts[3], *parts[2], *parts[1], *refs[2 * count:])

    half = count // 2
    return pl.pallas_call(
        kernel,
        out_shape=[jax.ShapeDtypeStruct((1, queries.shape[1]), jnp.float32)] * count,
        in_specs=[VMEM_SPEC] * (2 * count + 1),
        out_specs=[VMEM_SPEC] * count,
        compiler_params=LARGE,
        name="score",
    )(queries, *near[:half], *far[half:], *far[:half], *near[half:])


def swap(value, layer_bits, ex_bits):
    layers, examples = lax.axis_size("layer"), lax.axis_size("ex")
    pairs = [
        (l * examples + e, (l ^ layer_bits) * examples + (e ^ ex_bits))
        for l in range(layers) for e in range(examples)
    ]
    return lax.ppermute(value, ("layer", "ex"), pairs)


def doublings(size, start=1):
    bits = []
    while start < size:
        bits.append(start)
        start *= 2
    return bits


def on_device(acts, grads, proj_in, proj_out, queries):
    layers, examples = lax.axis_size("layer"), lax.axis_size("ex")
    tokens = acts.shape[2]
    other = swap(queries, 0, 1)
    low, full = outer_product(acts[0, 0], grads[0, 0], proj_in[0], proj_out[0])
    joint, *first, last = doublings(layers)
    for bit in first:
        full = full + swap(low, bit, 0).astype(jnp.float32)
        low = full.astype(jnp.bfloat16)
    blocks = spread(full, swap(low, last, 0), examples // 2)

    slots = {0: blocks}
    *outer, inner = reversed(doublings(examples, 2))
    for bit in outer:
        half = bit // 2
        kept = {}
        for m, held in slots.items():
            kept[m] = held[:half]
            kept[m ^ bit ^ 1] = [(come, come) for come in (swap(b, 0, bit | 1) for b, _ in held[half:])]
        slots = kept
    near, far = {}, {}
    for m, ((keep, keep_too), (give, give_too)) in slots.items():
        near[m], far[m] = keep, swap(keep_too, joint, 0)
        near[m ^ inner ^ 1], far[m ^ inner ^ 1] = swap(give, 0, inner | 1), swap(give_too, joint, inner | 1)
    names = list(slots) + [m ^ inner ^ 1 for m in slots]
    scores = score(turn(queries, other), [near[m] for m in names], [far[m] for m in names])
    parts = dict(zip(names, scores))
    for bit in reversed(doublings(examples, 2)):
        back = {m ^ bit ^ 1: swap(parts[m], 0, bit | 1) for m in parts if m & bit}
        parts = {m: parts[m] + back[m] for m in parts if not m & bit}
    return parts[0] * (1.0 / math.sqrt(tokens * layers))


def solution(mesh):
    placed = (
        P("layer", ("groups", "ex"), None, None),
        P("layer", ("groups", "ex"), None, None),
        P("layer", None, None),
        P("layer", None, None),
        P("layer", "ex"),
    )
    return jax.shard_map(
        on_device,
        mesh=mesh,
        in_specs=placed,
        out_specs=P(("groups", "ex"), "layer"),
        check_vma=False,
    )
```

time: 20.4 us -> 18.8 us (0.922)
  the two profiles are of different devices: /device:TPU:0 before, /device:TPU:1 now
where the time goes in v4:
time: 18.8 us; the launch traced here: 18.7 us
  starting transfers between devices  8.08 us (43%)
  waiting for transfers between devices  6.25 us (33%)
  Pallas kernels  3.79 us (20%)
  other arithmetic  0.51 us (3%)
    ppermute x6, starting transfers between devices, swap(): return lax.ppermute(value, ('layer', 'ex'), pairs)  8.08 us
    ppermute x6, waiting for transfers between devices, swap(): return lax.ppermute(value, ('layer', 'ex'), pairs)  6.25 us
    pallas_call x1, Pallas kernels, outer_product(): pl.pallas_call(outer_kernel, out_shape=(jax.ShapeDtypeStruct(shape, jnp.b...  2.81 us
    pallas_call x1, Pallas kernels, turn(): pl.pallas_call(turn_kernel, out_shape=jax.ShapeDtypeStruct((2 * own.shape...  0.59 us
    mul x1, other arithmetic, on_device(): return parts[0] * (1.0 / math.sqrt(tokens * layers))  0.51 us
    pallas_call x1, Pallas kernels, score(): pl.pallas_call(kernel, out_shape=[jax.ShapeDtypeStruct((1, queries.shape[...  0.38 us
  transfers between devices with their start and end apart: 6, of which 5 were waited for; matrix products, arithmetic and copies ran while one was open for 0% of the time, Pallas kernels for 18%

profile of v4, /device:TPU:1, one launch (start us, length us, event | category | flops | bytes accessed | tf_op | source)
XLA Modules:
  0.0 18.7 jit_solution(10994822511683335808)
XLA Ops:
  0.0 0.0 copy-start
  0.0 0.1 collective-permute-start
  0.1 2.8 %outer_product.1 = (bf16[128,128]{1,0:T(8,128)(2,1)S(1)}, f32[128,128]{1,0:T(8,128)S(1)}) custom-call(bf16[256,4096]{1,0:T(8,128)(2,1)} %bitcast.4, bf16[256,1024]{1,0:T(8,128)(2,1)} %bitcast.6, bf16[128,4096]{1,0:T(8,128)(2,1)} %bitcast.5, bf16[128,1024]{1,0:T(8,128)(2,1)} %bitcast.7), custom_call_target="tpu_custom_call" | custom-call | tf_op jit(solution)/shard_map/outer_product/pallas_call | solution.py:62
  2.9 3.8 %collective-permute-start.1 = (bf16[128,128]{1,0:T(8,128)(2,1)S(1)}, bf16[128,128]{1,0:T(8,128)(2,1)S(1)}, u32[]{:S(2)}, u32[]{:S(2)}) collective-permute-start(bf16[128,128]{1,0:T(8,128)(2,1)S(1)} %get-tuple-element.14), channel_id=1, source_target_pairs={{0,8},{1,9},{2,10},{3,11},{4,12},{5,13},{6,14},{7,15},{8,0},{9,1},... | collective-permute-start | bytes 98312 | tf_op jit(solution)/shard_map/ppermute | solution.py:159
  6.6 1.7 %collective-permute-done.1.refs_1_ = bf16[128,128]{1,0:T(8,128)(2,1)S(1)} collective-permute-done((bf16[128,128]{1,0:T(8,128)(2,1)S(1)}, bf16[128,128]{1,0:T(8,128)(2,1)S(1)}, u32[]{:S(2)}, u32[]{:S(2)}) %collective-permute-start.1) | collective-permute-done | bytes 32800 | tf_op jit(solution)/shard_map/ppermute | solution.py:159
  8.3 3.1 %collective-permute-start.2 = (bf16[64,128]{1,0:T(8,128)(2,1)S(1)}, bf16[64,128]{1,0:T(8,128)(2,1)S(1)}, u32[]{:S(2)}, u32[]{:S(2)}) collective-permute-start(bf16[64,128]{1,0:T(8,128)(2,1)S(1)} %get-tuple-element.16), channel_id=1, source_target_pairs={{0,7},{1,6},{2,5},{3,4},{4,3},{5,2},{6,1},{7,0},{8,15},{9,14},{10,... | collective-permute-start | bytes 49160 | tf_op jit(solution)/shard_map/ppermute | solution.py:159
  11.4 0.2 collective-permute-start.3
  11.6 0.5 %collective-permute-start.4 = (bf16[64,128]{1,0:T(8,128)(2,1)S(1)}, bf16[64,128]{1,0:T(8,128)(2,1)S(1)}, u32[]{:S(2)}, u32[]{:S(2)}) collective-permute-start(bf16[64,128]{1,0:T(8,128)(2,1)S(1)} %get-tuple-element.18), channel_id=1, source_target_pairs={{0,3},{1,2},{2,1},{3,0},{4,7},{5,6},{6,5},{7,4},{8,11},{9,10},{10,... | collective-permute-start | bytes 49160 | tf_op jit(solution)/shard_map/ppermute | solution.py:159
  12.0 0.0 collective-permute-done.other
  12.1 0.0 copy-done
  12.1 0.6 %turn.1.queries = bf16[8192,128]{1,0:T(8,128)(2,1)S(1)} custom-call(bf16[128,4096]{1,0:T(8,128)(2,1)S(1)} %copy-done, bf16[128,4096]{1,0:T(8,128)(2,1)S(1)} %collective-permute-done.other), custom_call_target="tpu_custom_call" | custom-call | tf_op jit(solution)/shard_map/turn/pallas_call | solution.py:104
  12.7 0.2 collective-permute-done.2.refs_1_
  12.8 1.2 %collective-permute-done.3.refs_2_ = bf16[64,128]{1,0:T(8,128)(2,1)S(1)} collective-permute-done((bf16[64,128]{1,0:T(8,128)(2,1)S(1)}, bf16[64,128]{1,0:T(8,128)(2,1)S(1)}, u32[]{:S(2)}, u32[]{:S(2)}) %collective-permute-start.3) | collective-permute-done | bytes 16416 | tf_op jit(solution)/shard_map/ppermute | solution.py:159
  14.0 0.7 %collective-permute-done.4.refs_3_ = bf16[64,128]{1,0:T(8,128)(2,1)S(1)} collective-permute-done((bf16[64,128]{1,0:T(8,128)(2,1)S(1)}, bf16[64,128]{1,0:T(8,128)(2,1)S(1)}, u32[]{:S(2)}, u32[]{:S(2)}) %collective-permute-start.4) | collective-permute-done | bytes 16416 | tf_op jit(solution)/shard_map/ppermute | solution.py:159
  14.7 0.4 %score.1 = (f32[1,128]{1,0:T(1,128)S(1)}, f32[1,128]{1,0:T(1,128)S(1)}) custom-call(bf16[8192,128]{1,0:T(8,128)(2,1)S(1)} %turn.1.queries, bf16[64,128]{1,0:T(8,128)(2,1)S(1)} %get-tuple-element.15.refs_0_, bf16[64,128]{1,0:T(8,128)(2,1)S(1)} %collective-permute-done.2.refs_1_, bf16[64,128]{1,0:T(8,128)(2,1)S(1)} %collective-permute-done.3.refs_2_, ...), custom_call_target="tpu_custom_call" | custom-call | tf_op jit(solution)/shard_map/score/pallas_call | solution.py:143
  15.1 0.5 %collective-permute-start.5 = (f32[1,128]{1,0:T(1,128)S(1)}, f32[1,128]{1,0:T(1,128)S(1)}, u32[]{:S(2)}, u32[]{:S(2)}) collective-permute-start(f32[1,128]{1,0:T(1,128)S(1)} %get-tuple-element.20), channel_id=1, source_target_pairs={{0,3},{1,2},{2,1},{3,0},{4,7},{5,6},{6,5},{7,4},{8,11},{9,10},{10,... | collective-permute-start | bytes 1544 | tf_op jit(solution)/shard_map/ppermute | solution.py:159
  15.7 2.5 %collective-permute-done.5 = f32[1,128]{1,0:T(1,128)S(1)} collective-permute-done((f32[1,128]{1,0:T(1,128)S(1)}, f32[1,128]{1,0:T(1,128)S(1)}, u32[]{:S(2)}, u32[]{:S(2)}) %collective-permute-start.5) | collective-permute-done | bytes 544 | tf_op jit(solution)/shard_map/ppermute | solution.py:159
  18.1 0.5 %add_multiply_fusion = f32[1,128]{1,0:T(1,128)} fusion(f32[1,128]{1,0:T(1,128)S(1)} %get-tuple-element.19, f32[1,128]{1,0:T(1,128)S(1)} %collective-permute-done.5), kind=kLoop, calls=%fused_computation | loop fusion | flops 256 | bytes 1536 | tf_op jit(solution)/shard_map/mul | solution.py:200
  (1 shorter events, 0.0 us)
Async XLA Ops:
  0.0 12.1 %copy-start = (bf16[128,4096]{1,0:T(8,128)(2,1)S(1)}, bf16[128,4096]{1,0:T(8,128)(2,1)}, u32[]{:S(2)}) copy-start(bf16[128,4096]{1,0:T(8,128)(2,1)} %own.1) | copy-start | bytes 3145732
  0.0 12.0 %collective-permute-start = (bf16[128,4096]{1,0:T(8,128)(2,1)}, bf16[128,4096]{1,0:T(8,128)(2,1)S(1)}, u32[]{:S(2)}, u32[]{:S(2)}) collective-permute-start(bf16[128,4096]{1,0:T(8,128)(2,1)} %own.1), channel_id=1, source_target_pairs={{0,1},{1,0},{2,3},{3,2},{4,5},{5,4},{6,7},{7,6},{8,9},{9,8},{10,11... | collective-permute-start | bytes 3145736 | tf_op jit(solution)/shard_map/ppermute | solution.py:159
  2.9 5.4 %collective-permute-start.1 = (bf16[128,128]{1,0:T(8,128)(2,1)S(1)}, bf16[128,128]{1,0:T(8,128)(2,1)S(1)}, u32[]{:S(2)}, u32[]{:S(2)}) collective-permute-start(bf16[128,128]{1,0:T(8,128)(2,1)S(1)} %get-tuple-element.14), channel_id=1, source_target_pairs={{0,8},{1,9},{2,10},{3,11},{4,12},{5,13},{6,14},{7,15},{8,0},{9,1},... | collective-permute-start | bytes 98312 | tf_op jit(solution)/shard_map/ppermute | solution.py:159
  8.3 4.5 %collective-permute-start.2 = (bf16[64,128]{1,0:T(8,128)(2,1)S(1)}, bf16[64,128]{1,0:T(8,128)(2,1)S(1)}, u32[]{:S(2)}, u32[]{:S(2)}) collective-permute-start(bf16[64,128]{1,0:T(8,128)(2,1)S(1)} %get-tuple-element.16), channel_id=1, source_target_pairs={{0,7},{1,6},{2,5},{3,4},{4,3},{5,2},{6,1},{7,0},{8,15},{9,14},{10,... | collective-permute-start | bytes 49160 | tf_op jit(solution)/shard_map/ppermute | solution.py:159
  11.4 2.6 %collective-permute-start.3 = (bf16[64,128]{1,0:T(8,128)(2,1)S(1)}, bf16[64,128]{1,0:T(8,128)(2,1)S(1)}, u32[]{:S(2)}, u32[]{:S(2)}) collective-permute-start(bf16[64,128]{1,0:T(8,128)(2,1)S(1)} %get-tuple-element.17), channel_id=1, source_target_pairs={{0,4},{1,5},{2,6},{3,7},{4,0},{5,1},{6,2},{7,3},{8,12},{9,13},{10,... | collective-permute-start | bytes 49160 | tf_op jit(solution)/shard_map/ppermute | solution.py:159
  11.6 3.2 %collective-permute-start.4 = (bf16[64,128]{1,0:T(8,128)(2,1)S(1)}, bf16[64,128]{1,0:T(8,128)(2,1)S(1)}, u32[]{:S(2)}, u32[]{:S(2)}) collective-permute-start(bf16[64,128]{1,0:T(8,128)(2,1)S(1)} %get-tuple-element.18), channel_id=1, source_target_pairs={{0,3},{1,2},{2,1},{3,0},{4,7},{5,6},{6,5},{7,4},{8,11},{9,10},{10,... | collective-permute-start | bytes 49160 | tf_op jit(solution)/shard_map/ppermute | solution.py:159
  15.1 3.0 %collective-permute-start.5 = (f32[1,128]{1,0:T(1,128)S(1)}, f32[1,128]{1,0:T(1,128)S(1)}, u32[]{:S(2)}, u32[]{:S(2)}) collective-permute-start(f32[1,128]{1,0:T(1,128)S(1)} %get-tuple-element.20), channel_id=1, source_target_pairs={{0,3},{1,2},{2,1},{3,0},{4,7},{5,6},{6,5},{7,4},{8,11},{9,10},{10,... | collective-permute-start | bytes 1544 | tf_op jit(solution)/shard_map/ppermute | solution.py:159

commit v5 on v4

--- a/solution.py
+++ b/solution.py
@@ -133,27 +133,29 @@
 
 def score(queries, near, far):
     count = len(near)
-
-    def kernel(queries, *refs):
-        half = count // 2
-        parts = [refs[k * half:(k + 1) * half] for k in range(4)]
-        score_kernel(count, queries, *parts[0], *parts[3], *parts[2], *parts[1], *refs[2 * count:])
-
-    half = count // 2
     return pl.pallas_call(
-        kernel,
+        lambda *refs: score_kernel(count, *refs),
         out_shape=[jax.ShapeDtypeStruct((1, queries.shape[1]), jnp.float32)] * count,
         in_specs=[VMEM_SPEC] * (2 * count + 1),
         out_specs=[VMEM_SPEC] * count,
         compiler_params=LARGE,
         name="score",
-    )(queries, *near[:half], *far[half:], *far[:half], *near[half:])
+    )(queries, *near, *far)
 
 
 def swap(value, layer_bits, ex_bits):
     layers, examples = lax.axis_size("layer"), lax.axis_size("ex")
     pairs = [
         (l * examples + e, (l ^ layer_bits) * examples + (e ^ ex_bits))
+        for l in range(layers) for e in range(examples)
+    ]
+    return lax.ppermute(value, ("layer", "ex"), pairs)
+
+
+def cross(value, early, layer_bits, ex_bits):
+    layers, examples = lax.axis_size("layer"), lax.axis_size("ex")
+    pairs = [
+        (l * examples + e, (l ^ layer_bits if (e % 4 == 2) == early else l) * examples + (e ^ ex_bits))
         for l in range(layers) for e in range(examples)
     ]
     return lax.ppermute(value, ("layer", "ex"), pairs)
@@ -190,10 +192,12 @@
     near, far = {}, {}
     for m, ((keep, keep_too), (give, give_too)) in slots.items():
         near[m], far[m] = keep, swap(keep_too, joint, 0)
-        near[m ^ inner ^ 1], far[m ^ inner ^ 1] = swap(give, 0, inner | 1), swap(give_too, joint, inner | 1)
+        near[m ^ inner ^ 1], far[m ^ inner ^ 1] = cross(give, False, joint, inner | 1), cross(give_too, True, joint, inner | 1)
     names = list(slots) + [m ^ inner ^ 1 for m in slots]
-    scores = score(turn(queries, other), [near[m] for m in names], [far[m] for m in names])
-    parts = dict(zip(names, scores))
+    table = turn(queries, other)
+    away = [m for m in names if m]
+    parts = dict(zip(away, score(table, [far[m] for m in away], [near[m] for m in away])))
+    (parts[0],) = score(table, [far[0]], [near[0]])
     for bit in reversed(doublings(examples, 2)):
         back = {m ^ bit ^ 1: swap(parts[m], 0, bit | 1) for m in parts if m & bit}
         parts = {m: parts[m] + back[m] for m in parts if not m & bit}

time: 18.8 us -> 17.7 us (0.941)
  the two profiles are of different devices: /device:TPU:1 before, /device:TPU:0 now
where the time goes in v5:
time: 17.7 us; the launch traced here: 17.6 us
  starting transfers between devices  8.8 us (50%)
  waiting for transfers between devices  4.13 us (23%)
  Pallas kernels  4.11 us (23%)
  other arithmetic  0.51 us (3%)
    ppermute x4, starting transfers between devices, swap(): return lax.ppermute(value, ('layer', 'ex'), pairs)  5.75 us
    ppermute x4, waiting for transfers between devices, swap(): return lax.ppermute(value, ('layer', 'ex'), pairs)  3.27 us
    ppermute x2, starting transfers between devices, cross(): return lax.ppermute(value, ('layer', 'ex'), pairs)  3.05 us
    pallas_call x1, Pallas kernels, outer_product(): pl.pallas_call(outer_kernel, out_shape=(jax.ShapeDtypeStruct(shape, jnp.b...  2.74 us
    ppermute x2, waiting for transfers between devices, cross(): return lax.ppermute(value, ('layer', 'ex'), pairs)  0.87 us
    pallas_call x2, Pallas kernels, score(): pl.pallas_call(lambda *refs: score_kernel(count, *refs), out_shape=[jax.S...  0.77 us
    pallas_call x1, Pallas kernels, turn(): pl.pallas_call(turn_kernel, out_shape=jax.ShapeDtypeStruct((2 * own.shape...  0.59 us
    mul x1, other arithmetic, on_device(): return parts[0] * (1.0 / math.sqrt(tokens * layers))  0.51 us
  transfers between devices with their start and end apart: 6, of which 4 were waited for; matrix products, arithmetic and copies ran while one was open for 0% of the time, Pallas kernels for 23%

profile of v5, /device:TPU:0, one launch (start us, length us, event | category | flops | bytes accessed | tf_op | source)
XLA Modules:
  0.0 17.6 jit_solution(15283950104098546844)
XLA Ops:
  0.0 0.0 copy-start
  0.0 0.5 %collective-permute-start = (bf16[128,4096]{1,0:T(8,128)(2,1)}, bf16[128,4096]{1,0:T(8,128)(2,1)S(1)}, u32[]{:S(2)}, u32[]{:S(2)}) collective-permute-start(bf16[128,4096]{1,0:T(8,128)(2,1)} %own.1), channel_id=1, source_target_pairs={{0,1},{1,0},{2,3},{3,2},{4,5},{5,4},{6,7},{7,6},{8,9},{9,8},{10,11... | collective-permute-start | bytes 3145736 | tf_op jit(solution)/shard_map/ppermute | solution.py:152
  0.5 2.7 %outer_product.1 = (bf16[128,128]{1,0:T(8,128)(2,1)S(1)}, f32[128,128]{1,0:T(8,128)S(1)}) custom-call(bf16[256,4096]{1,0:T(8,128)(2,1)} %bitcast.4, bf16[256,1024]{1,0:T(8,128)(2,1)} %bitcast.6, bf16[128,4096]{1,0:T(8,128)(2,1)} %bitcast.5, bf16[128,1024]{1,0:T(8,128)(2,1)} %bitcast.7), custom_call_target="tpu_custom_call" | custom-call | tf_op jit(solution)/shard_map/outer_product/pallas_call | solution.py:62
  3.2 3.7 %collective-permute-start.1 = (bf16[128,128]{1,0:T(8,128)(2,1)S(1)}, bf16[128,128]{1,0:T(8,128)(2,1)S(1)}, u32[]{:S(2)}, u32[]{:S(2)}) collective-permute-start(bf16[128,128]{1,0:T(8,128)(2,1)S(1)} %get-tuple-element.12), channel_id=1, source_target_pairs={{0,8},{1,9},{2,10},{3,11},{4,12},{5,13},{6,14},{7,15},{8,0},{9,1},... | collective-permute-start | bytes 98312 | tf_op jit(solution)/shard_map/ppermute | solution.py:152
  6.9 2.0 %collective-permute-done.1.refs_1_ = bf16[128,128]{1,0:T(8,128)(2,1)S(1)} collective-permute-done((bf16[128,128]{1,0:T(8,128)(2,1)S(1)}, bf16[128,128]{1,0:T(8,128)(2,1)S(1)}, u32[]{:S(2)}, u32[]{:S(2)}) %collective-permute-start.1) | collective-permute-done | bytes 32800 | tf_op jit(solution)/shard_map/ppermute | solution.py:152
  8.9 0.7 %collective-permute-start.3 = (bf16[64,128]{1,0:T(8,128)(2,1)S(1)}, bf16[64,128]{1,0:T(8,128)(2,1)S(1)}, u32[]{:S(2)}, u32[]{:S(2)}) collective-permute-start(bf16[64,128]{1,0:T(8,128)(2,1)S(1)} %get-tuple-element.15), channel_id=1, source_target_pairs={{0,3},{1,2},{2,5},{3,0},{4,7},{5,6},{6,1},{7,4},{8,11},{9,10},{10,... | collective-permute-start | bytes 49160 | tf_op jit(solution)/shard_map/ppermute | solution.py:161
  9.6 2.4 %collective-permute-start.4 = (bf16[64,128]{1,0:T(8,128)(2,1)S(1)}, bf16[64,128]{1,0:T(8,128)(2,1)S(1)}, u32[]{:S(2)}, u32[]{:S(2)}) collective-permute-start(bf16[64,128]{1,0:T(8,128)(2,1)S(1)} %get-tuple-element.16), channel_id=1, source_target_pairs={{0,7},{1,6},{2,1},{3,4},{4,3},{5,2},{6,5},{7,0},{8,15},{9,14},{10,... | collective-permute-start | bytes 49160 | tf_op jit(solution)/shard_map/ppermute | solution.py:161
  12.0 0.2 %collective-permute-start.2 = (bf16[64,128]{1,0:T(8,128)(2,1)S(1)}, bf16[64,128]{1,0:T(8,128)(2,1)S(1)}, u32[]{:S(2)}, u32[]{:S(2)}) collective-permute-start(bf16[64,128]{1,0:T(8,128)(2,1)S(1)} %get-tuple-element.13), channel_id=1, source_target_pairs={{0,4},{1,5},{2,6},{3,7},{4,0},{5,1},{6,2},{7,3},{8,12},{9,13},{10,... | collective-permute-start | bytes 49160 | tf_op jit(solution)/shard_map/ppermute | solution.py:152
  12.2 0.0 collective-permute-done.other
  12.2 0.0 copy-done
  12.2 0.6 %turn.1.refs_0_ = bf16[8192,128]{1,0:T(8,128)(2,1)S(1)} custom-call(bf16[128,4096]{1,0:T(8,128)(2,1)S(1)} %copy-done, bf16[128,4096]{1,0:T(8,128)(2,1)S(1)} %collective-permute-done.other), custom_call_target="tpu_custom_call" | custom-call | tf_op jit(solution)/shard_map/turn/pallas_call | solution.py:104
  12.8 0.0 collective-permute-done.3.refs_1_
  12.8 0.9 %collective-permute-done.4.refs_2_ = bf16[64,128]{1,0:T(8,128)(2,1)S(1)} collective-permute-done((bf16[64,128]{1,0:T(8,128)(2,1)S(1)}, bf16[64,128]{1,0:T(8,128)(2,1)S(1)}, u32[]{:S(2)}, u32[]{:S(2)}) %collective-permute-start.4) | collective-permute-done | bytes 16416 | tf_op jit(solution)/shard_map/ppermute | solution.py:161
  13.7 0.4 %score.3 = f32[1,128]{1,0:T(1,128)S(1)} custom-call(bf16[8192,128]{1,0:T(8,128)(2,1)S(1)} %turn.1.refs_0_, bf16[64,128]{1,0:T(8,128)(2,1)S(1)} %collective-permute-done.3.refs_1_, bf16[64,128]{1,0:T(8,128)(2,1)S(1)} %collective-permute-done.4.refs_2_), custom_call_target="tpu_custom_call" | custom-call | tf_op jit(solution)/shard_map/score/pallas_call | solution.py:136
  14.1 1.4 %collective-permute-start.5 = (f32[1,128]{1,0:T(1,128)S(1)}, f32[1,128]{1,0:T(1,128)S(1)}, u32[]{:S(2)}, u32[]{:S(2)}) collective-permute-start(f32[1,128]{1,0:T(1,128)S(1)} %score.3), channel_id=1, source_target_pairs={{0,3},{1,2},{2,1},{3,0},{4,7},{5,6},{6,5},{7,4},{8,11},{9,10},{10,... | collective-permute-start | bytes 1544 | tf_op jit(solution)/shard_map/ppermute | solution.py:152
  15.4 0.3 %collective-permute-done.2.refs_1_ = bf16[64,128]{1,0:T(8,128)(2,1)S(1)} collective-permute-done((bf16[64,128]{1,0:T(8,128)(2,1)S(1)}, bf16[64,128]{1,0:T(8,128)(2,1)S(1)}, u32[]{:S(2)}, u32[]{:S(2)}) %collective-permute-start.2) | collective-permute-done | bytes 16416 | tf_op jit(solution)/shard_map/ppermute | solution.py:152
  15.7 0.4 %score.2 = f32[1,128]{1,0:T(1,128)S(1)} custom-call(bf16[8192,128]{1,0:T(8,128)(2,1)S(1)} %turn.1.refs_0_, bf16[64,128]{1,0:T(8,128)(2,1)S(1)} %collective-permute-done.2.refs_1_, bf16[64,128]{1,0:T(8,128)(2,1)S(1)} %get-tuple-element.14.refs_2_), custom_call_target="tpu_custom_call" | custom-call | tf_op jit(solution)/shard_map/score/pallas_call | solution.py:136
  16.1 1.0 %collective-permute-done.5 = f32[1,128]{1,0:T(1,128)S(1)} collective-permute-done((f32[1,128]{1,0:T(1,128)S(1)}, f32[1,128]{1,0:T(1,128)S(1)}, u32[]{:S(2)}, u32[]{:S(2)}) %collective-permute-start.5) | collective-permute-done | bytes 544 | tf_op jit(solution)/shard_map/ppermute | solution.py:152
  17.1 0.5 %add_multiply_fusion = f32[1,128]{1,0:T(1,128)} fusion(f32[1,128]{1,0:T(1,128)S(1)} %score.2, f32[1,128]{1,0:T(1,128)S(1)} %collective-permute-done.5), kind=kLoop, calls=%fused_computation | loop fusion | flops 256 | bytes 1536 | tf_op jit(solution)/shard_map/mul | solution.py:204
  (1 shorter events, 0.0 us)
Async XLA Ops:
  0.0 12.2 %copy-start = (bf16[128,4096]{1,0:T(8,128)(2,1)S(1)}, bf16[128,4096]{1,0:T(8,128)(2,1)}, u32[]{:S(2)}) copy-start(bf16[128,4096]{1,0:T(8,128)(2,1)} %own.1) | copy-start | bytes 3145732
  0.0 12.2 %collective-permute-start = (bf16[128,4096]{1,0:T(8,128)(2,1)}, bf16[128,4096]{1,0:T(8,128)(2,1)S(1)}, u32[]{:S(2)}, u32[]{:S(2)}) collective-permute-start(bf16[128,4096]{1,0:T(8,128)(2,1)} %own.1), channel_id=1, source_target_pairs={{0,1},{1,0},{2,3},{3,2},{4,5},{5,4},{6,7},{7,6},{8,9},{9,8},{10,11... | collective-permute-start | bytes 3145736 | tf_op jit(solution)/shard_map/ppermute | solution.py:152
  3.2 5.7 %collective-permute-start.1 = (bf16[128,128]{1,0:T(8,128)(2,1)S(1)}, bf16[128,128]{1,0:T(8,128)(2,1)S(1)}, u32[]{:S(2)}, u32[]{:S(2)}) collective-permute-start(bf16[128,128]{1,0:T(8,128)(2,1)S(1)} %get-tuple-element.12), channel_id=1, source_target_pairs={{0,8},{1,9},{2,10},{3,11},{4,12},{5,13},{6,14},{7,15},{8,0},{9,1},... | collective-permute-start | bytes 98312 | tf_op jit(solution)/shard_map/ppermute | solution.py:152
  8.9 3.9 %collective-permute-start.3 = (bf16[64,128]{1,0:T(8,128)(2,1)S(1)}, bf16[64,128]{1,0:T(8,128)(2,1)S(1)}, u32[]{:S(2)}, u32[]{:S(2)}) collective-permute-start(bf16[64,128]{1,0:T(8,128)(2,1)S(1)} %get-tuple-element.15), channel_id=1, source_target_pairs={{0,3},{1,2},{2,5},{3,0},{4,7},{5,6},{6,1},{7,4},{8,11},{9,10},{10,... | collective-permute-start | bytes 49160 | tf_op jit(solution)/shard_map/ppermute | solution.py:161
  9.6 4.1 %collective-permute-start.4 = (bf16[64,128]{1,0:T(8,128)(2,1)S(1)}, bf16[64,128]{1,0:T(8,128)(2,1)S(1)}, u32[]{:S(2)}, u32[]{:S(2)}) collective-permute-start(bf16[64,128]{1,0:T(8,128)(2,1)S(1)} %get-tuple-element.16), channel_id=1, source_target_pairs={{0,7},{1,6},{2,1},{3,4},{4,3},{5,2},{6,5},{7,0},{8,15},{9,14},{10,... | collective-permute-start | bytes 49160 | tf_op jit(solution)/shard_map/ppermute | solution.py:161
  12.0 3.7 %collective-permute-start.2 = (bf16[64,128]{1,0:T(8,128)(2,1)S(1)}, bf16[64,128]{1,0:T(8,128)(2,1)S(1)}, u32[]{:S(2)}, u32[]{:S(2)}) collective-permute-start(bf16[64,128]{1,0:T(8,128)(2,1)S(1)} %get-tuple-element.13), channel_id=1, source_target_pairs={{0,4},{1,5},{2,6},{3,7},{4,0},{5,1},{6,2},{7,3},{8,12},{9,13},{10,... | collective-permute-start | bytes 49160 | tf_op jit(solution)/shard_map/ppermute | solution.py:152
  14.1 3.0 %collective-permute-start.5 = (f32[1,128]{1,0:T(1,128)S(1)}, f32[1,128]{1,0:T(1,128)S(1)}, u32[]{:S(2)}, u32[]{:S(2)}) collective-permute-start(f32[1,128]{1,0:T(1,128)S(1)} %score.3), channel_id=1, source_target_pairs={{0,3},{1,2},{2,1},{3,0},{4,7},{5,6},{6,5},{7,4},{8,11},{9,10},{10,... | collective-permute-start | bytes 1544 | tf_op jit(solution)/shard_map/ppermute | solution.py:152

commit v6 on v5

--- a/solution.py
+++ b/solution.py
@@ -20,7 +20,8 @@
     )
 
 
-def outer_kernel(acts, grads, proj_in, proj_out, low_ref, full_ref, a_buf, g_buf, pi_buf, po_buf, sems):
+def outer_kernel(count, acts, grads, proj_in, proj_out, low_own, low_rest, full_own, full_rest,
+                 total, a_buf, g_buf, pi_buf, po_buf, sems):
     width = acts.shape[1] // PIECES
 
     def piece(k):
@@ -52,19 +53,30 @@
     x_low = lax.fori_loop(
         0, PIECES, add_piece, jnp.zeros((acts.shape[0], proj_in.shape[0]), jnp.float32))
     outer = jnp.dot(g_low, x_low.astype(jnp.bfloat16), preferred_element_type=jnp.float32)
-    full_ref[...] = outer
-    low_ref[...] = outer.astype(jnp.bfloat16)
-
-
-def outer_product(*args):
+    total[...] = outer
+    place = lax.axis_index("ex") // 2
+    rows = total.shape[0] // count
+    for k in range(count):
+        block = total[pl.ds(pl.multiple_of((place ^ k) * rows, rows), rows), :]
+        if k == 0:
+            full_own[...] = block
+            low_own[...] = block.astype(jnp.bfloat16)
+        else:
+            full_rest[(k - 1) * rows:k * rows, :] = block
+            low_rest[(k - 1) * rows:k * rows, :] = block.astype(jnp.bfloat16)
+
+
+def outer_product(count, *args):
     acts, grads, proj_in, proj_out = args
-    shape = (proj_out.shape[0], proj_in.shape[0])
+    rows, width = proj_out.shape[0] // count, proj_in.shape[0]
+    rest = rows * (count - 1)
     return pl.pallas_call(
-        outer_kernel,
-        out_shape=(jax.ShapeDtypeStruct(shape, jnp.bfloat16), jax.ShapeDtypeStruct(shape, jnp.float32)),
+        lambda *refs: outer_kernel(count, *refs),
+        out_shape=[jax.ShapeDtypeStruct((n, width), t) for t in (jnp.bfloat16, jnp.float32) for n in (rows, rest)],
         in_specs=[HBM_SPEC] * 4,
-        out_specs=(VMEM_SPEC, VMEM_SPEC),
-        scratch_shapes=[pltpu.VMEM(a.shape, a.dtype) for a in args]
+        out_specs=[VMEM_SPEC] * 4,
+        scratch_shapes=[pltpu.VMEM((rows * count, width), jnp.float32)]
+        + [pltpu.VMEM(a.shape, a.dtype) for a in args]
         + [pltpu.SemaphoreType.DMA((2 + 2 * PIECES,))],
         compiler_params=LARGE,
         name="outer_product",
@@ -72,10 +84,9 @@
 
 
 def spread_kernel(count, own, got, *outs):
-    place = lax.axis_index("ex") // 2
     rows = own.shape[0] // count
     for k in range(count):
-        block = pl.ds(pl.multiple_of((place ^ k) * rows, rows), rows)
+        block = slice(k * rows, (k + 1) * rows)
         total = (own[block, :] + got[block, :].astype(jnp.float32)).astype(jnp.bfloat16)
         outs[k][...] = total
         outs[k + count][...] = total
@@ -173,12 +184,16 @@
     layers, examples = lax.axis_size("layer"), lax.axis_size("ex")
     tokens = acts.shape[2]
     other = swap(queries, 0, 1)
-    low, full = outer_product(acts[0, 0], grads[0, 0], proj_in[0], proj_out[0])
+    count = examples // 2
+    *low, full_own, full_rest = outer_product(count, acts[0, 0], grads[0, 0], proj_in[0], proj_out[0])
+    full = [full_own, full_rest]
     joint, *first, last = doublings(layers)
     for bit in first:
-        full = full + swap(low, bit, 0).astype(jnp.float32)
-        low = full.astype(jnp.bfloat16)
-    blocks = spread(full, swap(low, last, 0), examples // 2)
+        full = [f + swap(a, bit, 0).astype(jnp.float32) for a, f in zip(low, full)]
+        low = [f.astype(jnp.bfloat16) for f in full]
+    got, table = lax.optimization_barrier((swap(low[1], last, 0), turn(queries, other)))
+    rest = spread(full[1], got, count - 1)
+    blocks = spread(full[0], swap(low[0], last, 0), 1) + rest
 
     slots = {0: blocks}
     *outer, inner = reversed(doublings(examples, 2))
@@ -194,7 +209,6 @@
         near[m], far[m] = keep, swap(keep_too, joint, 0)
         near[m ^ inner ^ 1], far[m ^ inner ^ 1] = cross(give, False, joint, inner | 1), cross(give_too, True, joint, inner | 1)
     names = list(slots) + [m ^ inner ^ 1 for m in slots]
-    table = turn(queries, other)
     away = [m for m in names if m]
     parts = dict(zip(away, score(table, [far[m] for m in away], [near[m] for m in away])))
     (parts[0],) = score(table, [far[0]], [near[0]])

time: 17.7 us -> 17.6 us (level)
  waiting for transfers between devices: 4.13 us -> 2.51 us
  starting transfers between devices: 8.8 us -> 10.2 us
    ppermute x4 -> x5, starting transfers between devices: 5.75 us -> 7.11 us  [swap(): return lax.ppermute(value, ('layer', 'ex'), pairs)]
    ppermute x4 -> x5, waiting for transfers between devices: 3.27 us -> 2.24 us  [swap(): return lax.ppermute(value, ('layer', 'ex'), pairs)]
    ppermute x2, waiting for transfers between devices: 0.87 us -> 0.27 us  [cross(): return lax.ppermute(value, ('layer', 'ex'), pairs)]
  transfers between devices with their start and end apart: 6 -> 7, of which waited for: 4 -> 4; matrix products, arithmetic and copies ran while one was open for 0% -> 0% of each run, Pallas kernels for 23% -> 24%
where the time goes in v6:
time: 17.6 us; the launch traced here: 17.4 us
  starting transfers between devices  10.2 us (58%)
  Pallas kernels  4.12 us (23%)
  waiting for transfers between devices  2.51 us (14%)
  other arithmetic  0.51 us (3%)
    ppermute x5, starting transfers between devices, swap(): return lax.ppermute(value, ('layer', 'ex'), pairs)  7.11 us
    ppermute x2, starting transfers between devices, cross(): return lax.ppermute(value, ('layer', 'ex'), pairs)  3.13 us
    pallas_call x1, Pallas kernels, outer_product(): pl.pallas_call(lambda *refs: outer_kernel(count, *refs), out_shape=[jax.S...  2.75 us
    ppermute x5, waiting for transfers between devices, swap(): return lax.ppermute(value, ('layer', 'ex'), pairs)  2.24 us
    pallas_call x2, Pallas kernels, score(): pl.pallas_call(lambda *refs: score_kernel(count, *refs), out_shape=[jax.S...  0.77 us
    pallas_call x1, Pallas kernels, turn(): pl.pallas_call(turn_kernel, out_shape=jax.ShapeDtypeStruct((2 * own.shape...  0.59 us
    mul x1, other arithmetic, on_device(): return parts[0] * (1.0 / math.sqrt(tokens * layers))  0.51 us
  transfers between devices with their start and end apart: 7, of which 4 were waited for; matrix products, arithmetic and copies ran while one was open for 0% of the time, Pallas kernels for 24%

profile of v6, /device:TPU:0, one launch (start us, length us, event | category | flops | bytes accessed | tf_op | source)
XLA Modules:
  0.0 17.4 jit_solution(9789759911166577638)
XLA Ops:
  0.0 0.0 copy-start
  0.0 0.5 %collective-permute-start.1 = (bf16[128,4096]{1,0:T(8,128)(2,1)}, bf16[128,4096]{1,0:T(8,128)(2,1)S(1)}, u32[]{:S(2)}, u32[]{:S(2)}) collective-permute-start(bf16[128,4096]{1,0:T(8,128)(2,1)} %own.1), channel_id=1, source_target_pairs={{0,1},{1,0},{2,3},{3,2},{4,5},{5,4},{6,7},{7,6},{8,9},{9,8},{10,11... | collective-permute-start | bytes 3145736 | tf_op jit(solution)/shard_map/ppermute | solution.py:163
  0.5 2.8 %outer_product.1 = (bf16[64,128]{1,0:T(8,128)(2,1)S(1)}, bf16[64,128]{1,0:T(8,128)(2,1)S(1)}, f32[64,128]{1,0:T(8,128)S(1)}, f32[64,128]{1,0:T(8,128)S(1)}) custom-call(bf16[256,4096]{1,0:T(8,128)(2,1)} %bitcast.4, bf16[256,1024]{1,0:T(8,128)(2,1)} %bitcast.6, bf16[128,4096]{1,0:T(8,128)(2,1)} %bitcast.5, bf16[128,1024]{1,0:T(8,128)(2,1)} %bitcast.7), custom_call_target="tpu_custom_call" | custom-call | tf_op jit(solution)/shard_map/outer_product/pallas_call | solution.py:73
  3.2 3.7 %collective-permute-start = (bf16[64,128]{1,0:T(8,128)(2,1)S(1)}, bf16[64,128]{1,0:T(8,128)(2,1)S(1)}, u32[]{:S(2)}, u32[]{:S(2)}) collective-permute-start(bf16[64,128]{1,0:T(8,128)(2,1)S(1)} %get-tuple-element.15), channel_id=1, source_target_pairs={{0,8},{1,9},{2,10},{3,11},{4,12},{5,13},{6,14},{7,15},{8,0},{9,1},... | collective-permute-start | bytes 49160 | tf_op jit(solution)/shard_map/ppermute | solution.py:163
  6.9 0.1 collective-permute-start.2
  7.0 0.0 collective-permute-done.1.other
  7.0 0.0 copy-done
  7.0 0.6 %turn.1.refs_0_ = bf16[8192,128]{1,0:T(8,128)(2,1)S(1)} custom-call(bf16[128,4096]{1,0:T(8,128)(2,1)S(1)} %copy-done, bf16[128,4096]{1,0:T(8,128)(2,1)S(1)} %collective-permute-done.1.other), custom_call_target="tpu_custom_call" | custom-call | tf_op jit(solution)/shard_map/turn/pallas_call | solution.py:115
  7.6 1.0 %collective-permute-done.refs_1_ = bf16[64,128]{1,0:T(8,128)(2,1)S(1)} collective-permute-done((bf16[64,128]{1,0:T(8,128)(2,1)S(1)}, bf16[64,128]{1,0:T(8,128)(2,1)S(1)}, u32[]{:S(2)}, u32[]{:S(2)}) %collective-permute-start) | collective-permute-done | bytes 16416 | tf_op jit(solution)/shard_map/ppermute | solution.py:163
  8.7 0.8 %collective-permute-start.4 = (bf16[64,128]{1,0:T(8,128)(2,1)S(1)}, bf16[64,128]{1,0:T(8,128)(2,1)S(1)}, u32[]{:S(2)}, u32[]{:S(2)}) collective-permute-start(bf16[64,128]{1,0:T(8,128)(2,1)S(1)} %get-tuple-element.23), channel_id=1, source_target_pairs={{0,3},{1,2},{2,5},{3,0},{4,7},{5,6},{6,1},{7,4},{8,11},{9,10},{10,... | collective-permute-start | bytes 49160 | tf_op jit(solution)/shard_map/ppermute | solution.py:172
  9.4 2.4 %collective-permute-start.5 = (bf16[64,128]{1,0:T(8,128)(2,1)S(1)}, bf16[64,128]{1,0:T(8,128)(2,1)S(1)}, u32[]{:S(2)}, u32[]{:S(2)}) collective-permute-start(bf16[64,128]{1,0:T(8,128)(2,1)S(1)} %get-tuple-element.24), channel_id=1, source_target_pairs={{0,7},{1,6},{2,1},{3,4},{4,3},{5,2},{6,5},{7,0},{8,15},{9,14},{10,... | collective-permute-start | bytes 49160 | tf_op jit(solution)/shard_map/ppermute | solution.py:172
  11.8 0.0 collective-permute-done.2.refs_1_
  11.8 1.4 %collective-permute-start.3 = (bf16[64,128]{1,0:T(8,128)(2,1)S(1)}, bf16[64,128]{1,0:T(8,128)(2,1)S(1)}, u32[]{:S(2)}, u32[]{:S(2)}) collective-permute-start(bf16[64,128]{1,0:T(8,128)(2,1)S(1)} %get-tuple-element.19), channel_id=1, source_target_pairs={{0,4},{1,5},{2,6},{3,7},{4,0},{5,1},{6,2},{7,3},{8,12},{9,13},{10,... | collective-permute-start | bytes 49160 | tf_op jit(solution)/shard_map/ppermute | solution.py:163
  13.2 0.0 collective-permute-done.4.refs_1_
  13.2 0.3 %collective-permute-done.5.refs_2_ = bf16[64,128]{1,0:T(8,128)(2,1)S(1)} collective-permute-done((bf16[64,128]{1,0:T(8,128)(2,1)S(1)}, bf16[64,128]{1,0:T(8,128)(2,1)S(1)}, u32[]{:S(2)}, u32[]{:S(2)}) %collective-permute-start.5) | collective-permute-done | bytes 16416 | tf_op jit(solution)/shard_map/ppermute | solution.py:172
  13.5 0.4 %score.3 = f32[1,128]{1,0:T(1,128)S(1)} custom-call(bf16[8192,128]{1,0:T(8,128)(2,1)S(1)} %turn.1.refs_0_, bf16[64,128]{1,0:T(8,128)(2,1)S(1)} %collective-permute-done.4.refs_1_, bf16[64,128]{1,0:T(8,128)(2,1)S(1)} %collective-permute-done.5.refs_2_), custom_call_target="tpu_custom_call" | custom-call | tf_op jit(solution)/shard_map/score/pallas_call | solution.py:147
  13.9 1.4 %collective-permute-start.6 = (f32[1,128]{1,0:T(1,128)S(1)}, f32[1,128]{1,0:T(1,128)S(1)}, u32[]{:S(2)}, u32[]{:S(2)}) collective-permute-start(f32[1,128]{1,0:T(1,128)S(1)} %score.3), channel_id=1, source_target_pairs={{0,3},{1,2},{2,1},{3,0},{4,7},{5,6},{6,5},{7,4},{8,11},{9,10},{10,... | collective-permute-start | bytes 1544 | tf_op jit(solution)/shard_map/ppermute | solution.py:163
  15.3 0.3 %collective-permute-done.3.refs_1_ = bf16[64,128]{1,0:T(8,128)(2,1)S(1)} collective-permute-done((bf16[64,128]{1,0:T(8,128)(2,1)S(1)}, bf16[64,128]{1,0:T(8,128)(2,1)S(1)}, u32[]{:S(2)}, u32[]{:S(2)}) %collective-permute-start.3) | collective-permute-done | bytes 16416 | tf_op jit(solution)/shard_map/ppermute | solution.py:163
  15.6 0.4 %score.2 = f32[1,128]{1,0:T(1,128)S(1)} custom-call(bf16[8192,128]{1,0:T(8,128)(2,1)S(1)} %turn.1.refs_0_, bf16[64,128]{1,0:T(8,128)(2,1)S(1)} %collective-permute-done.3.refs_1_, bf16[64,128]{1,0:T(8,128)(2,1)S(1)} %get-tuple-element.20.refs_2_), custom_call_target="tpu_custom_call" | custom-call | tf_op jit(solution)/shard_map/score/pallas_call | solution.py:147
  16.0 0.9 %collective-permute-done.6 = f32[1,128]{1,0:T(1,128)S(1)} collective-permute-done((f32[1,128]{1,0:T(1,128)S(1)}, f32[1,128]{1,0:T(1,128)S(1)}, u32[]{:S(2)}, u32[]{:S(2)}) %collective-permute-start.6) | collective-permute-done | bytes 544 | tf_op jit(solution)/shard_map/ppermute | solution.py:163
  16.9 0.5 %add_multiply_fusion = f32[1,128]{1,0:T(1,128)} fusion(f32[1,128]{1,0:T(1,128)S(1)} %score.2, f32[1,128]{1,0:T(1,128)S(1)} %collective-permute-done.6), kind=kLoop, calls=%fused_computation | loop fusion | flops 256 | bytes 1536 | tf_op jit(solution)/shard_map/mul | solution.py:218
  (2 shorter events, 0.0 us)
Async XLA Ops:
  0.0 7.0 %copy-start = (bf16[128,4096]{1,0:T(8,128)(2,1)S(1)}, bf16[128,4096]{1,0:T(8,128)(2,1)}, u32[]{:S(2)}) copy-start(bf16[128,4096]{1,0:T(8,128)(2,1)} %own.1) | copy-start | bytes 3145732
  0.0 7.0 %collective-permute-start.1 = (bf16[128,4096]{1,0:T(8,128)(2,1)}, bf16[128,4096]{1,0:T(8,128)(2,1)S(1)}, u32[]{:S(2)}, u32[]{:S(2)}) collective-permute-start(bf16[128,4096]{1,0:T(8,128)(2,1)} %own.1), channel_id=1, source_target_pairs={{0,1},{1,0},{2,3},{3,2},{4,5},{5,4},{6,7},{7,6},{8,9},{9,8},{10,11... | collective-permute-start | bytes 3145736 | tf_op jit(solution)/shard_map/ppermute | solution.py:163
  3.2 5.5 %collective-permute-start = (bf16[64,128]{1,0:T(8,128)(2,1)S(1)}, bf16[64,128]{1,0:T(8,128)(2,1)S(1)}, u32[]{:S(2)}, u32[]{:S(2)}) collective-permute-start(bf16[64,128]{1,0:T(8,128)(2,1)S(1)} %get-tuple-element.15), channel_id=1, source_target_pairs={{0,8},{1,9},{2,10},{3,11},{4,12},{5,13},{6,14},{7,15},{8,0},{9,1},... | collective-permute-start | bytes 49160 | tf_op jit(solution)/shard_map/ppermute | solution.py:163
  6.9 4.9 %collective-permute-start.2 = (bf16[64,128]{1,0:T(8,128)(2,1)S(1)}, bf16[64,128]{1,0:T(8,128)(2,1)S(1)}, u32[]{:S(2)}, u32[]{:S(2)}) collective-permute-start(bf16[64,128]{1,0:T(8,128)(2,1)S(1)} %get-tuple-element.18), channel_id=1, source_target_pairs={{0,8},{1,9},{2,10},{3,11},{4,12},{5,13},{6,14},{7,15},{8,0},{9,1},... | collective-permute-start | bytes 49160 | tf_op jit(solution)/shard_map/ppermute | solution.py:163
  8.7 4.6 %collective-permute-start.4 = (bf16[64,128]{1,0:T(8,128)(2,1)S(1)}, bf16[64,128]{1,0:T(8,128)(2,1)S(1)}, u32[]{:S(2)}, u32[]{:S(2)}) collective-permute-start(bf16[64,128]{1,0:T(8,128)(2,1)S(1)} %get-tuple-element.23), channel_id=1, source_target_pairs={{0,3},{1,2},{2,5},{3,0},{4,7},{5,6},{6,1},{7,4},{8,11},{9,10},{10,... | collective-permute-start | bytes 49160 | tf_op jit(solution)/shard_map/ppermute | solution.py:172
  9.4 4.1 %collective-permute-start.5 = (bf16[64,128]{1,0:T(8,128)(2,1)S(1)}, bf16[64,128]{1,0:T(8,128)(2,1)S(1)}, u32[]{:S(2)}, u32[]{:S(2)}) collective-permute-start(bf16[64,128]{1,0:T(8,128)(2,1)S(1)} %get-tuple-element.24), channel_id=1, source_target_pairs={{0,7},{1,6},{2,1},{3,4},{4,3},{5,2},{6,5},{7,0},{8,15},{9,14},{10,... | collective-permute-start | bytes 49160 | tf_op jit(solution)/shard_map/ppermute | solution.py:172
  11.8 3.8 %collective-permute-start.3 = (bf16[64,128]{1,0:T(8,128)(2,1)S(1)}, bf16[64,128]{1,0:T(8,128)(2,1)S(1)}, u32[]{:S(2)}, u32[]{:S(2)}) collective-permute-start(bf16[64,128]{1,0:T(8,128)(2,1)S(1)} %get-tuple-element.19), channel_id=1, source_target_pairs={{0,4},{1,5},{2,6},{3,7},{4,0},{5,1},{6,2},{7,3},{8,12},{9,13},{10,... | collective-permute-start | bytes 49160 | tf_op jit(solution)/shard_map/ppermute | solution.py:163
  13.9 3.0 %collective-permute-start.6 = (f32[1,128]{1,0:T(1,128)S(1)}, f32[1,128]{1,0:T(1,128)S(1)}, u32[]{:S(2)}, u32[]{:S(2)}) collective-permute-start(f32[1,128]{1,0:T(1,128)S(1)} %score.3), channel_id=1, source_target_pairs={{0,3},{1,2},{2,1},{3,0},{4,7},{5,6},{6,5},{7,4},{8,11},{9,10},{10,... | collective-permute-start | bytes 1544 | tf_op jit(solution)/shard_map/ppermute | solution.py:163

commit v7 on v6

--- a/solution.py
+++ b/solution.py
@@ -27,8 +27,8 @@
     def piece(k):
         cols = pl.ds(k * width if isinstance(k, int) else pl.multiple_of(k * width, width), width)
         return cols, (
+            pltpu.make_async_copy(acts.at[:, cols], a_buf.at[:, cols], sems.at[3 + 2 * k]),
             pltpu.make_async_copy(proj_in.at[:, cols], pi_buf.at[:, cols], sems.at[2 + 2 * k]),
-            pltpu.make_async_copy(acts.at[:, cols], a_buf.at[:, cols], sems.at[3 + 2 * k]),
         )
 
     out_copies = (

time: 17.6 us -> 17.5 us (level)
  no operation moved by 1% of the time
where the time goes in v7:
time: 17.5 us; the launch traced here: 17.4 us
  starting transfers between devices  10.2 us (58%)
  Pallas kernels  4.09 us (23%)
  waiting for transfers between devices  2.52 us (14%)
  other arithmetic  0.51 us (3%)
    ppermute x5, starting transfers between devices, swap(): return lax.ppermute(value, ('layer', 'ex'), pairs)  7.1 us
    ppermute x2, starting transfers between devices, cross(): return lax.ppermute(value, ('layer', 'ex'), pairs)  3.13 us
    pallas_call x1, Pallas kernels, outer_product(): pl.pallas_call(lambda *refs: outer_kernel(count, *refs), out_shape=[jax.S...  2.72 us
    ppermute x5, waiting for transfers between devices, swap(): return lax.ppermute(value, ('layer', 'ex'), pairs)  2.25 us
    pallas_call x2, Pallas kernels, score(): pl.pallas_call(lambda *refs: score_kernel(count, *refs), out_shape=[jax.S...  0.77 us
    pallas_call x1, Pallas kernels, turn(): pl.pallas_call(turn_kernel, out_shape=jax.ShapeDtypeStruct((2 * own.shape...  0.59 us
    mul x1, other arithmetic, on_device(): return parts[0] * (1.0 / math.sqrt(tokens * layers))  0.51 us
  transfers between devices with their start and end apart: 7, of which 4 were waited for; matrix products, arithmetic and copies ran while one was open for 0% of the time, Pallas kernels for 24%

profile of v7, /device:TPU:0, one launch (start us, length us, event | category | flops | bytes accessed | tf_op | source)
XLA Modules:
  0.0 17.4 jit_solution(1134455147845314155)
XLA Ops:
  0.0 0.0 copy-start
  0.0 0.5 %collective-permute-start.1 = (bf16[128,4096]{1,0:T(8,128)(2,1)}, bf16[128,4096]{1,0:T(8,128)(2,1)S(1)}, u32[]{:S(2)}, u32[]{:S(2)}) collective-permute-start(bf16[128,4096]{1,0:T(8,128)(2,1)} %own.1), channel_id=1, source_target_pairs={{0,1},{1,0},{2,3},{3,2},{4,5},{5,4},{6,7},{7,6},{8,9},{9,8},{10,11... | collective-permute-start | bytes 3145736 | tf_op jit(solution)/shard_map/ppermute | solution.py:163
  0.5 2.7 %outer_product.1 = (bf16[64,128]{1,0:T(8,128)(2,1)S(1)}, bf16[64,128]{1,0:T(8,128)(2,1)S(1)}, f32[64,128]{1,0:T(8,128)S(1)}, f32[64,128]{1,0:T(8,128)S(1)}) custom-call(bf16[256,4096]{1,0:T(8,128)(2,1)} %bitcast.4, bf16[256,1024]{1,0:T(8,128)(2,1)} %bitcast.6, bf16[128,4096]{1,0:T(8,128)(2,1)} %bitcast.5, bf16[128,1024]{1,0:T(8,128)(2,1)} %bitcast.7), custom_call_target="tpu_custom_call" | custom-call | tf_op jit(solution)/shard_map/outer_product/pallas_call | solution.py:73
  3.2 3.7 %collective-permute-start = (bf16[64,128]{1,0:T(8,128)(2,1)S(1)}, bf16[64,128]{1,0:T(8,128)(2,1)S(1)}, u32[]{:S(2)}, u32[]{:S(2)}) collective-permute-start(bf16[64,128]{1,0:T(8,128)(2,1)S(1)} %get-tuple-element.15), channel_id=1, source_target_pairs={{0,8},{1,9},{2,10},{3,11},{4,12},{5,13},{6,14},{7,15},{8,0},{9,1},... | collective-permute-start | bytes 49160 | tf_op jit(solution)/shard_map/ppermute | solution.py:163
  6.9 0.1 collective-permute-start.2
  7.0 0.0 collective-permute-done.1.other
  7.0 0.0 copy-done
  7.0 0.6 %turn.1.refs_0_ = bf16[8192,128]{1,0:T(8,128)(2,1)S(1)} custom-call(bf16[128,4096]{1,0:T(8,128)(2,1)S(1)} %copy-done, bf16[128,4096]{1,0:T(8,128)(2,1)S(1)} %collective-permute-done.1.other), custom_call_target="tpu_custom_call" | custom-call | tf_op jit(solution)/shard_map/turn/pallas_call | solution.py:115
  7.6 1.0 %collective-permute-done.refs_1_ = bf16[64,128]{1,0:T(8,128)(2,1)S(1)} collective-permute-done((bf16[64,128]{1,0:T(8,128)(2,1)S(1)}, bf16[64,128]{1,0:T(8,128)(2,1)S(1)}, u32[]{:S(2)}, u32[]{:S(2)}) %collective-permute-start) | collective-permute-done | bytes 16416 | tf_op jit(solution)/shard_map/ppermute | solution.py:163
  8.7 0.8 %collective-permute-start.4 = (bf16[64,128]{1,0:T(8,128)(2,1)S(1)}, bf16[64,128]{1,0:T(8,128)(2,1)S(1)}, u32[]{:S(2)}, u32[]{:S(2)}) collective-permute-start(bf16[64,128]{1,0:T(8,128)(2,1)S(1)} %get-tuple-element.23), channel_id=1, source_target_pairs={{0,3},{1,2},{2,5},{3,0},{4,7},{5,6},{6,1},{7,4},{8,11},{9,10},{10,... | collective-permute-start | bytes 49160 | tf_op jit(solution)/shard_map/ppermute | solution.py:172
  9.4 2.4 %collective-permute-start.5 = (bf16[64,128]{1,0:T(8,128)(2,1)S(1)}, bf16[64,128]{1,0:T(8,128)(2,1)S(1)}, u32[]{:S(2)}, u32[]{:S(2)}) collective-permute-start(bf16[64,128]{1,0:T(8,128)(2,1)S(1)} %get-tuple-element.24), channel_id=1, source_target_pairs={{0,7},{1,6},{2,1},{3,4},{4,3},{5,2},{6,5},{7,0},{8,15},{9,14},{10,... | collective-permute-start | bytes 49160 | tf_op jit(solution)/shard_map/ppermute | solution.py:172
  11.8 0.0 collective-permute-done.2.refs_1_
  11.8 1.4 %collective-permute-start.3 = (bf16[64,128]{1,0:T(8,128)(2,1)S(1)}, bf16[64,128]{1,0:T(8,128)(2,1)S(1)}, u32[]{:S(2)}, u32[]{:S(2)}) collective-permute-start(bf16[64,128]{1,0:T(8,128)(2,1)S(1)} %get-tuple-element.19), channel_id=1, source_target_pairs={{0,4},{1,5},{2,6},{3,7},{4,0},{5,1},{6,2},{7,3},{8,12},{9,13},{10,... | collective-permute-start | bytes 49160 | tf_op jit(solution)/shard_map/ppermute | solution.py:163
  13.2 0.0 collective-permute-done.4.refs_1_
  13.2 0.3 %collective-permute-done.5.refs_2_ = bf16[64,128]{1,0:T(8,128)(2,1)S(1)} collective-permute-done((bf16[64,128]{1,0:T(8,128)(2,1)S(1)}, bf16[64,128]{1,0:T(8,128)(2,1)S(1)}, u32[]{:S(2)}, u32[]{:S(2)}) %collective-permute-start.5) | collective-permute-done | bytes 16416 | tf_op jit(solution)/shard_map/ppermute | solution.py:172
  13.5 0.4 %score.3 = f32[1,128]{1,0:T(1,128)S(1)} custom-call(bf16[8192,128]{1,0:T(8,128)(2,1)S(1)} %turn.1.refs_0_, bf16[64,128]{1,0:T(8,128)(2,1)S(1)} %collective-permute-done.4.refs_1_, bf16[64,128]{1,0:T(8,128)(2,1)S(1)} %collective-permute-done.5.refs_2_), custom_call_target="tpu_custom_call" | custom-call | tf_op jit(solution)/shard_map/score/pallas_call | solution.py:147
  13.9 1.4 %collective-permute-start.6 = (f32[1,128]{1,0:T(1,128)S(1)}, f32[1,128]{1,0:T(1,128)S(1)}, u32[]{:S(2)}, u32[]{:S(2)}) collective-permute-start(f32[1,128]{1,0:T(1,128)S(1)} %score.3), channel_id=1, source_target_pairs={{0,3},{1,2},{2,1},{3,0},{4,7},{5,6},{6,5},{7,4},{8,11},{9,10},{10,... | collective-permute-start | bytes 1544 | tf_op jit(solution)/shard_map/ppermute | solution.py:163
  15.3 0.3 %collective-permute-done.3.refs_1_ = bf16[64,128]{1,0:T(8,128)(2,1)S(1)} collective-permute-done((bf16[64,128]{1,0:T(8,128)(2,1)S(1)}, bf16[64,128]{1,0:T(8,128)(2,1)S(1)}, u32[]{:S(2)}, u32[]{:S(2)}) %collective-permute-start.3) | collective-permute-done | bytes 16416 | tf_op jit(solution)/shard_map/ppermute | solution.py:163
  15.6 0.4 %score.2 = f32[1,128]{1,0:T(1,128)S(1)} custom-call(bf16[8192,128]{1,0:T(8,128)(2,1)S(1)} %turn.1.refs_0_, bf16[64,128]{1,0:T(8,128)(2,1)S(1)} %collective-permute-done.3.refs_1_, bf16[64,128]{1,0:T(8,128)(2,1)S(1)} %get-tuple-element.20.refs_2_), custom_call_target="tpu_custom_call" | custom-call | tf_op jit(solution)/shard_map/score/pallas_call | solution.py:147
  16.0 0.9 %collective-permute-done.6 = f32[1,128]{1,0:T(1,128)S(1)} collective-permute-done((f32[1,128]{1,0:T(1,128)S(1)}, f32[1,128]{1,0:T(1,128)S(1)}, u32[]{:S(2)}, u32[]{:S(2)}) %collective-permute-start.6) | collective-permute-done | bytes 544 | tf_op jit(solution)/shard_map/ppermute | solution.py:163
  16.9 0.5 %add_multiply_fusion = f32[1,128]{1,0:T(1,128)} fusion(f32[1,128]{1,0:T(1,128)S(1)} %score.2, f32[1,128]{1,0:T(1,128)S(1)} %collective-permute-done.6), kind=kLoop, calls=%fused_computation | loop fusion | flops 256 | bytes 1536 | tf_op jit(solution)/shard_map/mul | solution.py:218
  (2 shorter events, 0.0 us)
Async XLA Ops:
  0.0 7.0 %copy-start = (bf16[128,4096]{1,0:T(8,128)(2,1)S(1)}, bf16[128,4096]{1,0:T(8,128)(2,1)}, u32[]{:S(2)}) copy-start(bf16[128,4096]{1,0:T(8,128)(2,1)} %own.1) | copy-start | bytes 3145732
  0.0 7.0 %collective-permute-start.1 = (bf16[128,4096]{1,0:T(8,128)(2,1)}, bf16[128,4096]{1,0:T(8,128)(2,1)S(1)}, u32[]{:S(2)}, u32[]{:S(2)}) collective-permute-start(bf16[128,4096]{1,0:T(8,128)(2,1)} %own.1), channel_id=1, source_target_pairs={{0,1},{1,0},{2,3},{3,2},{4,5},{5,4},{6,7},{7,6},{8,9},{9,8},{10,11... | collective-permute-start | bytes 3145736 | tf_op jit(solution)/shard_map/ppermute | solution.py:163
  3.2 5.5 %collective-permute-start = (bf16[64,128]{1,0:T(8,128)(2,1)S(1)}, bf16[64,128]{1,0:T(8,128)(2,1)S(1)}, u32[]{:S(2)}, u32[]{:S(2)}) collective-permute-start(bf16[64,128]{1,0:T(8,128)(2,1)S(1)} %get-tuple-element.15), channel_id=1, source_target_pairs={{0,8},{1,9},{2,10},{3,11},{4,12},{5,13},{6,14},{7,15},{8,0},{9,1},... | collective-permute-start | bytes 49160 | tf_op jit(solution)/shard_map/ppermute | solution.py:163
  6.9 4.9 %collective-permute-start.2 = (bf16[64,128]{1,0:T(8,128)(2,1)S(1)}, bf16[64,128]{1,0:T(8,128)(2,1)S(1)}, u32[]{:S(2)}, u32[]{:S(2)}) collective-permute-start(bf16[64,128]{1,0:T(8,128)(2,1)S(1)} %get-tuple-element.18), channel_id=1, source_target_pairs={{0,8},{1,9},{2,10},{3,11},{4,12},{5,13},{6,14},{7,15},{8,0},{9,1},... | collective-permute-start | bytes 49160 | tf_op jit(solution)/shard_map/ppermute | solution.py:163
  8.7 4.6 %collective-permute-start.4 = (bf16[64,128]{1,0:T(8,128)(2,1)S(1)}, bf16[64,128]{1,0:T(8,128)(2,1)S(1)}, u32[]{:S(2)}, u32[]{:S(2)}) collective-permute-start(bf16[64,128]{1,0:T(8,128)(2,1)S(1)} %get-tuple-element.23), channel_id=1, source_target_pairs={{0,3},{1,2},{2,5},{3,0},{4,7},{5,6},{6,1},{7,4},{8,11},{9,10},{10,... | collective-permute-start | bytes 49160 | tf_op jit(solution)/shard_map/ppermute | solution.py:172
  9.4 4.1 %collective-permute-start.5 = (bf16[64,128]{1,0:T(8,128)(2,1)S(1)}, bf16[64,128]{1,0:T(8,128)(2,1)S(1)}, u32[]{:S(2)}, u32[]{:S(2)}) collective-permute-start(bf16[64,128]{1,0:T(8,128)(2,1)S(1)} %get-tuple-element.24), channel_id=1, source_target_pairs={{0,7},{1,6},{2,1},{3,4},{4,3},{5,2},{6,5},{7,0},{8,15},{9,14},{10,... | collective-permute-start | bytes 49160 | tf_op jit(solution)/shard_map/ppermute | solution.py:172
  11.8 3.8 %collective-permute-start.3 = (bf16[64,128]{1,0:T(8,128)(2,1)S(1)}, bf16[64,128]{1,0:T(8,128)(2,1)S(1)}, u32[]{:S(2)}, u32[]{:S(2)}) collective-permute-start(bf16[64,128]{1,0:T(8,128)(2,1)S(1)} %get-tuple-element.19), channel_id=1, source_target_pairs={{0,4},{1,5},{2,6},{3,7},{4,0},{5,1},{6,2},{7,3},{8,12},{9,13},{10,... | collective-permute-start | bytes 49160 | tf_op jit(solution)/shard_map/ppermute | solution.py:163
  13.9 3.0 %collective-permute-start.6 = (f32[1,128]{1,0:T(1,128)S(1)}, f32[1,128]{1,0:T(1,128)S(1)}, u32[]{:S(2)}, u32[]{:S(2)}) collective-permute-start(f32[1,128]{1,0:T(1,128)S(1)} %score.3), channel_id=1, source_target_pairs={{0,3},{1,2},{2,1},{3,0},{4,7},{5,6},{6,5},{7,4},{8,11},{9,10},{10,... | collective-permute-start | bytes 1544 | tf_op jit(solution)/shard_map/ppermute | solution.py:163

commit v8 on v7

--- a/solution.py
+++ b/solution.py
@@ -187,11 +187,12 @@
     count = examples // 2
     *low, full_own, full_rest = outer_product(count, acts[0, 0], grads[0, 0], proj_in[0], proj_out[0])
     full = [full_own, full_rest]
+    low[1], late_queries = lax.optimization_barrier((low[1], queries))
     joint, *first, last = doublings(layers)
     for bit in first:
         full = [f + swap(a, bit, 0).astype(jnp.float32) for a, f in zip(low, full)]
         low = [f.astype(jnp.bfloat16) for f in full]
-    got, table = lax.optimization_barrier((swap(low[1], last, 0), turn(queries, other)))
+    got, table = lax.optimization_barrier((swap(low[1], last, 0), turn(late_queries, other)))
     rest = spread(full[1], got, count - 1)
     blocks = spread(full[0], swap(low[0], last, 0), 1) + rest
 

time: 17.5 us -> 17.5 us (level)
  no operation moved by 1% of the time
where the time goes in v8:
time: 17.5 us; the launch traced here: 17.4 us
  starting transfers between devices  10.2 us (58%)
  Pallas kernels  4.09 us (23%)
  waiting for transfers between devices  2.52 us (14%)
  other arithmetic  0.51 us (3%)
    ppermute x5, starting transfers between devices, swap(): return lax.ppermute(value, ('layer', 'ex'), pairs)  7.1 us
    ppermute x2, starting transfers between devices, cross(): return lax.ppermute(value, ('layer', 'ex'), pairs)  3.13 us
    pallas_call x1, Pallas kernels, outer_product(): pl.pallas_call(lambda *refs: outer_kernel(count, *refs), out_shape=[jax.S...  2.72 us
    ppermute x5, waiting for transfers between devices, swap(): return lax.ppermute(value, ('layer', 'ex'), pairs)  2.25 us
    pallas_call x2, Pallas kernels, score(): pl.pallas_call(lambda *refs: score_kernel(count, *refs), out_shape=[jax.S...  0.77 us
    pallas_call x1, Pallas kernels, turn(): pl.pallas_call(turn_kernel, out_shape=jax.ShapeDtypeStruct((2 * own.shape...  0.59 us
    mul x1, other arithmetic, on_device(): return parts[0] * (1.0 / math.sqrt(tokens * layers))  0.51 us
  transfers between devices with their start and end apart: 7, of which 4 were waited for; matrix products, arithmetic and copies ran while one was open for 0% of the time, Pallas kernels for 24%

profile of v8, /device:TPU:0, one launch (start us, length us, event | category | flops | bytes accessed | tf_op | source)
XLA Modules:
  0.0 17.4 jit_solution(1134455147845314155)
XLA Ops:
  0.0 0.0 copy-start
  0.0 0.5 %collective-permute-start.1 = (bf16[128,4096]{1,0:T(8,128)(2,1)}, bf16[128,4096]{1,0:T(8,128)(2,1)S(1)}, u32[]{:S(2)}, u32[]{:S(2)}) collective-permute-start(bf16[128,4096]{1,0:T(8,128)(2,1)} %own), channel_id=1, source_target_pairs={{0,1},{1,0},{2,3},{3,2},{4,5},{5,4},{6,7},{7,6},{8,9},{9,8},{10,11... | collective-permute-start | bytes 3145736 | tf_op jit(solution)/shard_map/ppermute | solution.py:163
  0.5 2.7 %outer_product.1 = (bf16[64,128]{1,0:T(8,128)(2,1)S(1)}, bf16[64,128]{1,0:T(8,128)(2,1)S(1)}, f32[64,128]{1,0:T(8,128)S(1)}, f32[64,128]{1,0:T(8,128)S(1)}) custom-call(bf16[256,4096]{1,0:T(8,128)(2,1)} %bitcast.4, bf16[256,1024]{1,0:T(8,128)(2,1)} %bitcast.6, bf16[128,4096]{1,0:T(8,128)(2,1)} %bitcast.5, bf16[128,1024]{1,0:T(8,128)(2,1)} %bitcast.7), custom_call_target="tpu_custom_call" | custom-call | tf_op jit(solution)/shard_map/outer_product/pallas_call | solution.py:73
  3.2 3.7 %collective-permute-start = (bf16[64,128]{1,0:T(8,128)(2,1)S(1)}, bf16[64,128]{1,0:T(8,128)(2,1)S(1)}, u32[]{:S(2)}, u32[]{:S(2)}) collective-permute-start(bf16[64,128]{1,0:T(8,128)(2,1)S(1)} %get-tuple-element.18), channel_id=1, source_target_pairs={{0,8},{1,9},{2,10},{3,11},{4,12},{5,13},{6,14},{7,15},{8,0},{9,1},... | collective-permute-start | bytes 49160 | tf_op jit(solution)/shard_map/ppermute | solution.py:163
  6.9 0.1 collective-permute-start.2
  7.0 0.0 collective-permute-done.1.other
  7.0 0.0 copy-done
  7.0 0.6 %turn.1.refs_0_ = bf16[8192,128]{1,0:T(8,128)(2,1)S(1)} custom-call(bf16[128,4096]{1,0:T(8,128)(2,1)S(1)} %copy-done, bf16[128,4096]{1,0:T(8,128)(2,1)S(1)} %collective-permute-done.1.other), custom_call_target="tpu_custom_call" | custom-call | tf_op jit(solution)/shard_map/turn/pallas_call | solution.py:115
  7.6 1.0 %collective-permute-done.refs_1_ = bf16[64,128]{1,0:T(8,128)(2,1)S(1)} collective-permute-done((bf16[64,128]{1,0:T(8,128)(2,1)S(1)}, bf16[64,128]{1,0:T(8,128)(2,1)S(1)}, u32[]{:S(2)}, u32[]{:S(2)}) %collective-permute-start) | collective-permute-done | bytes 16416 | tf_op jit(solution)/shard_map/ppermute | solution.py:163
  8.7 0.8 %collective-permute-start.4 = (bf16[64,128]{1,0:T(8,128)(2,1)S(1)}, bf16[64,128]{1,0:T(8,128)(2,1)S(1)}, u32[]{:S(2)}, u32[]{:S(2)}) collective-permute-start(bf16[64,128]{1,0:T(8,128)(2,1)S(1)} %get-tuple-element.27), channel_id=1, source_target_pairs={{0,3},{1,2},{2,5},{3,0},{4,7},{5,6},{6,1},{7,4},{8,11},{9,10},{10,... | collective-permute-start | bytes 49160 | tf_op jit(solution)/shard_map/ppermute | solution.py:172
  9.4 2.4 %collective-permute-start.5 = (bf16[64,128]{1,0:T(8,128)(2,1)S(1)}, bf16[64,128]{1,0:T(8,128)(2,1)S(1)}, u32[]{:S(2)}, u32[]{:S(2)}) collective-permute-start(bf16[64,128]{1,0:T(8,128)(2,1)S(1)} %get-tuple-element.28), channel_id=1, source_target_pairs={{0,7},{1,6},{2,1},{3,4},{4,3},{5,2},{6,5},{7,0},{8,15},{9,14},{10,... | collective-permute-start | bytes 49160 | tf_op jit(solution)/shard_map/ppermute | solution.py:172
  11.8 0.0 collective-permute-done.2.refs_1_
  11.8 1.4 %collective-permute-start.3 = (bf16[64,128]{1,0:T(8,128)(2,1)S(1)}, bf16[64,128]{1,0:T(8,128)(2,1)S(1)}, u32[]{:S(2)}, u32[]{:S(2)}) collective-permute-start(bf16[64,128]{1,0:T(8,128)(2,1)S(1)} %get-tuple-element.23), channel_id=1, source_target_pairs={{0,4},{1,5},{2,6},{3,7},{4,0},{5,1},{6,2},{7,3},{8,12},{9,13},{10,... | collective-permute-start | bytes 49160 | tf_op jit(solution)/shard_map/ppermute | solution.py:163
  13.2 0.0 collective-permute-done.4.refs_1_
  13.2 0.3 %collective-permute-done.5.refs_2_ = bf16[64,128]{1,0:T(8,128)(2,1)S(1)} collective-permute-done((bf16[64,128]{1,0:T(8,128)(2,1)S(1)}, bf16[64,128]{1,0:T(8,128)(2,1)S(1)}, u32[]{:S(2)}, u32[]{:S(2)}) %collective-permute-start.5) | collective-permute-done | bytes 16416 | tf_op jit(solution)/shard_map/ppermute | solution.py:172
  13.5 0.4 %score.3 = f32[1,128]{1,0:T(1,128)S(1)} custom-call(bf16[8192,128]{1,0:T(8,128)(2,1)S(1)} %turn.1.refs_0_, bf16[64,128]{1,0:T(8,128)(2,1)S(1)} %collective-permute-done.4.refs_1_, bf16[64,128]{1,0:T(8,128)(2,1)S(1)} %collective-permute-done.5.refs_2_), custom_call_target="tpu_custom_call" | custom-call | tf_op jit(solution)/shard_map/score/pallas_call | solution.py:147
  13.9 1.4 %collective-permute-start.6 = (f32[1,128]{1,0:T(1,128)S(1)}, f32[1,128]{1,0:T(1,128)S(1)}, u32[]{:S(2)}, u32[]{:S(2)}) collective-permute-start(f32[1,128]{1,0:T(1,128)S(1)} %score.3), channel_id=1, source_target_pairs={{0,3},{1,2},{2,1},{3,0},{4,7},{5,6},{6,5},{7,4},{8,11},{9,10},{10,... | collective-permute-start | bytes 1544 | tf_op jit(solution)/shard_map/ppermute | solution.py:163
  15.3 0.3 %collective-permute-done.3.refs_1_ = bf16[64,128]{1,0:T(8,128)(2,1)S(1)} collective-permute-done((bf16[64,128]{1,0:T(8,128)(2,1)S(1)}, bf16[64,128]{1,0:T(8,128)(2,1)S(1)}, u32[]{:S(2)}, u32[]{:S(2)}) %collective-permute-start.3) | collective-permute-done | bytes 16416 | tf_op jit(solution)/shard_map/ppermute | solution.py:163
  15.6 0.4 %score.2 = f32[1,128]{1,0:T(1,128)S(1)} custom-call(bf16[8192,128]{1,0:T(8,128)(2,1)S(1)} %turn.1.refs_0_, bf16[64,128]{1,0:T(8,128)(2,1)S(1)} %collective-permute-done.3.refs_1_, bf16[64,128]{1,0:T(8,128)(2,1)S(1)} %get-tuple-element.24.refs_2_), custom_call_target="tpu_custom_call" | custom-call | tf_op jit(solution)/shard_map/score/pallas_call | solution.py:147
  16.0 0.9 %collective-permute-done.6 = f32[1,128]{1,0:T(1,128)S(1)} collective-permute-done((f32[1,128]{1,0:T(1,128)S(1)}, f32[1,128]{1,0:T(1,128)S(1)}, u32[]{:S(2)}, u32[]{:S(2)}) %collective-permute-start.6) | collective-permute-done | bytes 544 | tf_op jit(solution)/shard_map/ppermute | solution.py:163
  16.9 0.5 %add_multiply_fusion = f32[1,128]{1,0:T(1,128)} fusion(f32[1,128]{1,0:T(1,128)S(1)} %score.2, f32[1,128]{1,0:T(1,128)S(1)} %collective-permute-done.6), kind=kLoop, calls=%fused_computation | loop fusion | flops 256 | bytes 1536 | tf_op jit(solution)/shard_map/mul | solution.py:219
  (2 shorter events, 0.0 us)
Async XLA Ops:
  0.0 7.0 %copy-start = (bf16[128,4096]{1,0:T(8,128)(2,1)S(1)}, bf16[128,4096]{1,0:T(8,128)(2,1)}, u32[]{:S(2)}) copy-start(bf16[128,4096]{1,0:T(8,128)(2,1)} %own) | copy-start | bytes 3145732
  0.0 7.0 %collective-permute-start.1 = (bf16[128,4096]{1,0:T(8,128)(2,1)}, bf16[128,4096]{1,0:T(8,128)(2,1)S(1)}, u32[]{:S(2)}, u32[]{:S(2)}) collective-permute-start(bf16[128,4096]{1,0:T(8,128)(2,1)} %own), channel_id=1, source_target_pairs={{0,1},{1,0},{2,3},{3,2},{4,5},{5,4},{6,7},{7,6},{8,9},{9,8},{10,11... | collective-permute-start | bytes 3145736 | tf_op jit(solution)/shard_map/ppermute | solution.py:163
  3.2 5.5 %collective-permute-start = (bf16[64,128]{1,0:T(8,128)(2,1)S(1)}, bf16[64,128]{1,0:T(8,128)(2,1)S(1)}, u32[]{:S(2)}, u32[]{:S(2)}) collective-permute-start(bf16[64,128]{1,0:T(8,128)(2,1)S(1)} %get-tuple-element.18), channel_id=1, source_target_pairs={{0,8},{1,9},{2,10},{3,11},{4,12},{5,13},{6,14},{7,15},{8,0},{9,1},... | collective-permute-start | bytes 49160 | tf_op jit(solution)/shard_map/ppermute | solution.py:163
  6.9 4.9 %collective-permute-start.2 = (bf16[64,128]{1,0:T(8,128)(2,1)S(1)}, bf16[64,128]{1,0:T(8,128)(2,1)S(1)}, u32[]{:S(2)}, u32[]{:S(2)}) collective-permute-start(bf16[64,128]{1,0:T(8,128)(2,1)S(1)} %get-tuple-element.22), channel_id=1, source_target_pairs={{0,8},{1,9},{2,10},{3,11},{4,12},{5,13},{6,14},{7,15},{8,0},{9,1},... | collective-permute-start | bytes 49160 | tf_op jit(solution)/shard_map/ppermute | solution.py:163
  8.7 4.6 %collective-permute-start.4 = (bf16[64,128]{1,0:T(8,128)(2,1)S(1)}, bf16[64,128]{1,0:T(8,128)(2,1)S(1)}, u32[]{:S(2)}, u32[]{:S(2)}) collective-permute-start(bf16[64,128]{1,0:T(8,128)(2,1)S(1)} %get-tuple-element.27), channel_id=1, source_target_pairs={{0,3},{1,2},{2,5},{3,0},{4,7},{5,6},{6,1},{7,4},{8,11},{9,10},{10,... | collective-permute-start | bytes 49160 | tf_op jit(solution)/shard_map/ppermute | solution.py:172
  9.4 4.1 %collective-permute-start.5 = (bf16[64,128]{1,0:T(8,128)(2,1)S(1)}, bf16[64,128]{1,0:T(8,128)(2,1)S(1)}, u32[]{:S(2)}, u32[]{:S(2)}) collective-permute-start(bf16[64,128]{1,0:T(8,128)(2,1)S(1)} %get-tuple-element.28), channel_id=1, source_target_pairs={{0,7},{1,6},{2,1},{3,4},{4,3},{5,2},{6,5},{7,0},{8,15},{9,14},{10,... | collective-permute-start | bytes 49160 | tf_op jit(solution)/shard_map/ppermute | solution.py:172
  11.8 3.8 %collective-permute-start.3 = (bf16[64,128]{1,0:T(8,128)(2,1)S(1)}, bf16[64,128]{1,0:T(8,128)(2,1)S(1)}, u32[]{:S(2)}, u32[]{:S(2)}) collective-permute-start(bf16[64,128]{1,0:T(8,128)(2,1)S(1)} %get-tuple-element.23), channel_id=1, source_target_pairs={{0,4},{1,5},{2,6},{3,7},{4,0},{5,1},{6,2},{7,3},{8,12},{9,13},{10,... | collective-permute-start | bytes 49160 | tf_op jit(solution)/shard_map/ppermute | solution.py:163
  13.9 3.0 %collective-permute-start.6 = (f32[1,128]{1,0:T(1,128)S(1)}, f32[1,128]{1,0:T(1,128)S(1)}, u32[]{:S(2)}, u32[]{:S(2)}) collective-permute-start(f32[1,128]{1,0:T(1,128)S(1)} %score.3), channel_id=1, source_target_pairs={{0,3},{1,2},{2,1},{3,0},{4,7},{5,6},{6,5},{7,4},{8,11},{9,10},{10,... | collective-permute-start | bytes 1544 | tf_op jit(solution)/shard_map/ppermute | solution.py:163
